TPU v7x, 32 devices: a whole 2x2x4 slice. The times are simulated.
32 devices in a mesh: section: 4 (over z), dp: 8 (over y, x, core).
Axes of the slice: x: 2, y: 2, z: 4, core: 2. Of those that a mesh axis runs over, the one named last changes fastest.
Arguments:
- tokens: bfloat16 [2048, 4096], P('dp'), may hold values from -48 to 48
- orig_weight: bfloat16 [1024, 4096], P(('section', 'dp')), may hold values from -6 to 6
- keep_flags: int32 [64], replicated, may hold values from 0 to 1, as said below
Outputs:
- corrected: bfloat16 [1024, 4096], P(('section', 'dp'))
Inputs may be any that keep to these rules, and one draw needn't show every extreme that they name: `keep_flags`: exactly 12 of the 64 flags are 1.
All inputs are finite; a program needn't handle non-finite values.
Results may differ from a plain program's by a relative error of at most 0.003.
Values may be sent and summed in bfloat16 or wider, within the bound.
No kernel may reach another device: no remote copies, remote signals or barrier semaphores. Data moves between devices by JAX's collectives and lax.ppermute only.
A program may use at most 64 MiB of HBM per device.

v0:
```python
import jax
import jax.numpy as jnp
from jax import lax
from jax.sharding import PartitionSpec as P

KEEP_BLK = 12


def on_device(tokens, orig_weight, keep_flags):
    highest = lax.Precision.HIGHEST
    feature_count = tokens.shape[1]
    blocks = jnp.nonzero(keep_flags, size=KEEP_BLK)[0].astype(jnp.int32)
    kept_index = (
        (blocks[:, None] * 64 + jnp.arange(64, dtype=jnp.int32)[None, :])
        .reshape(-1)
        .astype(jnp.int32)
    )
    kept_tokens = jnp.take(tokens, kept_index, axis=1)
    kept_count = kept_tokens.shape[1]
    wide_tokens = tokens.astype(jnp.float32)
    partial_value = jnp.dot(kept_tokens.T, kept_tokens, preferred_element_type=jnp.float32)
    squares = jnp.sum(wide_tokens * wide_tokens)
    gramian, total_squares = lax.psum((partial_value, squares), "dp")
    damping = 0.01 * total_squares / feature_count
    system = gramian + damping * jnp.eye(kept_count, dtype=jnp.float32)
    factor = jnp.linalg.cholesky(system)
    projected = jnp.dot(
        tokens,
        lax.all_gather(orig_weight, "dp", axis=0, tiled=True).T,
        preferred_element_type=jnp.float32,
    )
    partial_right = jnp.dot(kept_tokens.astype(jnp.float32).T, projected, precision=highest)
    right_own = lax.psum_scatter(partial_right, "dp", scatter_dimension=1, tiled=True)
    solution = jax.scipy.linalg.cho_solve((factor, True), right_own)
    corrected = (
        jnp.zeros((orig_weight.shape[0], feature_count), jnp.float32)
        .at[:, kept_index]
        .set(solution.T)
    )
    return corrected.astype(jnp.bfloat16)


def solution(mesh):
    in_specs = (P("dp", None), P(("section", "dp"), None), P())
    out_specs = P(("section", "dp"), None)
    return jax.shard_map(
        on_device, mesh=mesh, in_specs=in_specs, out_specs=out_specs, check_vma=False
    )
```

profile of v0, /device:TPU:0, one launch (start us, length us, event | category | flops | bytes accessed | tf_op | source)
XLA Modules:
  0.0 342.4 jit_solution(4564168765014580789)
XLA Ops:
  6.5 0.7 fusion.80
  7.2 1.3 fusion.81
  8.8 1.0 scatter_custom_fusion
  10.0 0.7 fusion.79
  10.9 3.3 copy.41
  14.2 2.7 gather_fusion
  16.9 2.0 fusion.19
  19.0 0.7 all-gather.2.cloned.1.call-update
  19.7 1.7 multiply_reduce_fusion
  22.0 16.1 %psum.15 = f32[]{:T(128)} all-reduce(f32[]{:T(128)} %multiply_reduce_fusion), channel_id=1, replica_groups=mesh['section'=4,'dp'=8] {'dp'}, use_global_device_ids=true, to_apply=%region_6.7 | all-reduce | flops 1 | bytes 8 | tf_op jit(solution)/shard_map/psum | solution.py:23
  38.8 46.0 %all-reduce.3.cloned.1.call-done = f32[768,768]{0,1:T(8,128)} async-done(((f32[768,768]{0,1:T(8,128)}), f32[768,768]{0,1:T(8,128)}) %all-reduce.3.cloned.1.call-update) | async-done | bytes 2359312 | tf_op jit(solution)/shard_map/psum | solution.py:23
  84.8 3.3 select_add_fusion
  88.0 3.7 %copy.43 = f32[768,768]{1,0:T(8,128)} copy(f32[768,768]{0,1:T(8,128)} %select_add_fusion) | data formatting | bytes 4718592 | tf_op jit(solution)/shard_map/add | solution.py:25
  91.7 2.1 fusion
  93.8 1.4 copy-done.3
  95.2 11.7 %cholesky.164 = f32[128,128]{1,0:T(8,128)S(1)} custom-call(f32[128,128]{1,0:T(8,128)S(1)} %cholesky.421), custom_call_target="Cholesky" | custom-call | tf_op jit(solution)/shard_map/jit(cholesky)/cholesky | solution.py:26
  107.1 9.8 %custom-call.50 = f32[1,128,128]{1,2,0:T(8,128)S(1)} custom-call(f32[1,128,128]{2,1,0:T(8,128)S(1)} %get-tuple-element.44), custom_call_target="InvertDiagBlocksLowerTriangular" | custom-call | tf_op jit(solution)/shard_map/jit(cholesky)/cholesky | solution.py:26
  116.9 1.4 fusion.9
  118.4 1.4 convolution_subtract_fusion
  119.9 11.7 %cholesky.187 = f32[128,128]{1,0:T(8,128)S(1)} custom-call(f32[128,128]{1,0:T(8,128)S(1)} %cholesky.425), custom_call_target="Cholesky" | custom-call | tf_op jit(solution)/shard_map/jit(cholesky)/cholesky | solution.py:26
  131.7 10.6 %custom-call.51 = f32[1,128,128]{1,2,0:T(8,128)} custom-call(f32[1,128,128]{2,1,0:T(8,128)S(1)} %get-tuple-element.42), custom_call_target="InvertDiagBlocksLowerTriangular" | custom-call | tf_op jit(solution)/shard_map/jit(cholesky)/cholesky | solution.py:26
  142.5 0.6 copy-done.4
  143.5 1.9 convolution_subtract_fusion.1
  145.5 11.7 %cholesky.352 = f32[128,128]{1,0:T(8,128)S(1)} custom-call(f32[128,128]{1,0:T(8,128)S(1)} %cholesky.430), custom_call_target="Cholesky" | custom-call | tf_op jit(solution)/shard_map/jit(cholesky)/cholesky | solution.py:26
  157.4 9.8 %custom-call.52 = f32[1,128,128]{1,2,0:T(8,128)S(1)} custom-call(f32[1,128,128]{2,1,0:T(8,128)S(1)} %get-tuple-element.40), custom_call_target="InvertDiagBlocksLowerTriangular" | custom-call | tf_op jit(solution)/shard_map/jit(cholesky)/cholesky | solution.py:26
  167.6 2.1 convolution_subtract_fusion.2
  169.7 11.9 %cholesky.371 = f32[128,128]{1,0:T(8,128)S(1)} custom-call(f32[128,128]{1,0:T(8,128)S(1)} %cholesky.435), custom_call_target="Cholesky" | custom-call | tf_op jit(solution)/shard_map/jit(cholesky)/cholesky | solution.py:26
  181.7 9.8 %custom-call.53 = f32[1,128,128]{1,2,0:T(8,128)S(1)} custom-call(f32[1,128,128]{2,1,0:T(8,128)S(1)} %get-tuple-element.38), custom_call_target="InvertDiagBlocksLowerTriangular" | custom-call | tf_op jit(solution)/shard_map/jit(cholesky)/cholesky | solution.py:26
  191.9 1.9 convolution_subtract_fusion.3
  193.8 11.7 %cholesky.390 = f32[128,128]{1,0:T(8,128)S(1)} custom-call(f32[128,128]{1,0:T(8,128)S(1)} %cholesky.440), custom_call_target="Cholesky" | custom-call | tf_op jit(solution)/shard_map/jit(cholesky)/cholesky | solution.py:26
  205.7 9.8 %custom-call.54 = f32[1,128,128]{1,2,0:T(8,128)S(1)} custom-call(f32[1,128,128]{2,1,0:T(8,128)S(1)} %get-tuple-element.36), custom_call_target="InvertDiagBlocksLowerTriangular" | custom-call | tf_op jit(solution)/shard_map/jit(cholesky)/cholesky | solution.py:26
  215.8 1.9 convolution_subtract_fusion.4
  217.7 11.7 %cholesky.408 = f32[128,128]{1,0:T(8,128)S(1)} custom-call(f32[128,128]{1,0:T(8,128)S(1)} %convolution_subtract_fusion.4), custom_call_target="Cholesky" | custom-call | tf_op jit(solution)/shard_map/jit(cholesky)/cholesky | solution.py:26
  229.5 0.7 compare_reduce_fusion.4
  231.6 0.6 compare_reduce_fusion.3
  232.9 0.6 compare_reduce_fusion.2
  234.2 0.6 compare_reduce_fusion.1
  235.5 0.6 compare_reduce_fusion
  236.8 1.6 select_select_fusion
  238.4 3.1 fusion.93
  241.5 1.6 fusion.20
  243.2 17.0 %while.1 = (s32[]{:T(128)}, f32[768,768]{0,1:T(8,128)S(1)}, s32[6,2]{0,1:T(2,128)S(1)}, f32[6,128,128]{2,1,0:T(8,128)}, s32[]{:T(128)}) while((s32[]{:T(128)}, f32[768,768]{0,1:T(8,128)S(1)}, s32[6,2]{0,1:T(2,128)S(1)}, f32[6,128,128]{2,1,0:T(8,128)}, s32[]{:T(128)}) %tuple.43), condition=%wide.while_cond, body=%wide.while_body.sunk | while | flops 2 | bytes 393329 | solution.py:34
  243.3 0.6 fusion.114
  243.9 1.4 dynamic-slice.7
  245.4 0.6 bitcast_dynamic-update-slice_fusion.2
  246.7 1.4 dynamic-slice.7
  248.2 0.6 bitcast_dynamic-update-slice_fusion.2
  249.5 1.4 dynamic-slice.7
  251.1 0.6 bitcast_dynamic-update-slice_fusion.2
  252.3 1.4 dynamic-slice.7
  253.9 0.6 bitcast_dynamic-update-slice_fusion.2
  255.2 1.4 dynamic-slice.7
  256.7 0.6 bitcast_dynamic-update-slice_fusion.2
  258.0 1.4 dynamic-slice.7
  259.5 0.6 bitcast_dynamic-update-slice_fusion.2
  260.2 59.8 %custom-call.55 = f32[6,128,128]{1,2,0:T(8,128)S(1)} custom-call(f32[6,128,128]{2,1,0:T(8,128)} %get-tuple-element.12), custom_call_target="InvertDiagBlocksLowerTriangular" | custom-call | tf_op jit(solution)/shard_map/jit(_cho_solve)/triangular_solve | solution.py:34
  319.9 0.9 constant_dynamic-update-slice_fusion.4
  320.8 0.9 convolution_subtract_fusion.12
  321.9 0.9 convolution_subtract_fusion.11
  323.0 1.0 convolution_subtract_fusion.10
  324.1 1.0 convolution_subtract_fusion.9
  325.3 1.0 convolution_subtract_fusion.14
  329.8 4.8 %scatter_custom_fusion.1 = f32[32,4096]{0,1:T(8,128)S(1)} fusion(s32[768]{0:T(1024)S(1)} %fusion.77, f32[768,32]{1,0:T(8,128)S(1)} %copy.56, f32[]{:T(128)} %constant.267.clone.1), kind=kCustom, calls=%fused_computation.32 | custom fusion | bytes 524292 | tf_op jit(solution)/shard_map/scatter | solution.py:38
  334.6 1.0 copy.57
  (103 shorter events, 11.9 us)
Async XLA Ops:
  6.5 78.2 %all-reduce.3.cloned.1.call-start = ((), (), s32[]{:S(2)}) async-start(), calls=%async_computation.1 | async-start | bytes 4718592 | tf_op jit(solution)/shard_map/psum | solution.py:23
  16.9 2.9 copy-start
  18.9 219.5 %all-gather.2.cloned.1.call-start = ((), (), s32[]{:S(2)}) async-start(), calls=%async_computation.2 | async-start | bytes 2359296 | tf_op jit(solution)/shard_map/all_gather | solution.py:29
  19.7 300.3 %reduce-scatter.2.cloned.1.call-start = ((), (), s32[]{:S(2)}) async-start(), calls=%async_computation.3 | async-start | bytes 884736 | tf_op jit(solution)/shard_map/reduce_scatter | solution.py:33
  88.0 3.7 %copy-start.1 = (f32[768,768]{0,1:T(8,128)S(1)}, f32[768,768]{0,1:T(8,128)}, u32[]{:S(2)}) copy-start(f32[768,768]{0,1:T(8,128)} %all-reduce.3.cloned.1.call-done) | copy-start | bytes 7077892
  93.8 1.4 copy-start.3
  142.3 0.8 copy-start.4
  238.4 4.8 %copy-start.5 = (s32[6]{0:T(128)S(1)}, s32[6]{0:T(128)}, u32[]{:S(2)}) copy-start(s32[6]{0:T(128)} %iota_multiply_fusion) | copy-start | bytes 76
  238.4 4.8 %copy-start.2 = (f32[768,768]{0,1:T(8,128)S(1)}, f32[768,768]{0,1:T(8,128)}, u32[]{:S(2)}) copy-start(f32[768,768]{0,1:T(8,128)} %select_select_fusion) | copy-start | bytes 7077892
Sparse Core Ops, SparseCore 0:
  19.0 65.6 all-reduce.2
  86.8 27.4 all-gather.1
  243.3 34.4 reduce-scatter.1
where the time goes:
time: 347 us; the launch traced here: 342 us
  other arithmetic  197 us (57%)
  waiting for transfers between devices  46.8 us (13%)
  local copies, waits for them, and re-layouts  35.9 us (10%)
  matrix products  28.1 us (8%)
  between operations  18.5 us (5%)
  blocking collectives  16.1 us (5%)
    another operation x22, other arithmetic, on_device(): factor = jnp.linalg.cholesky(system)  124 us
    another operation x3, other arithmetic, on_device(): solution = jax.scipy.linalg.cho_solve((factor, True), right_own)  61.9 us
    psum x1, waiting for transfers between devices, on_device(): gramian, total_squares = lax.psum((partial_value, squares), 'dp')  46 us
    another operation x31, local copies, waits for them, and re-layouts  17 us
    psum x1, blocking collectives, on_device(): gramian, total_squares = lax.psum((partial_value, squares), 'dp')  16.1 us
    another operation x10, matrix products, on_device(): factor = jnp.linalg.cholesky(system)  12 us
    another operation x22, matrix products, on_device(): solution = jax.scipy.linalg.cho_solve((factor, True), right_own)  9.34 us
  transfers between devices with their start and end apart: 3, of which 1 were waited for; matrix products, arithmetic and copies ran while one was open for 66% of the time, Pallas kernels for 0%

commit v1 on v0

v1 whole, which is shorter than its diff:
```python
import jax
import jax.numpy as jnp
from jax import lax
from jax.experimental import pallas as pl
from jax.experimental.pallas import tpu as pltpu
from jax.sharding import PartitionSpec as P

KEEP_BLK = 12
PANEL = 128
SUB = 8
EXTRA = 16
VMEM_LIMIT = 56 * 1024 * 1024
NT = (((1,), (1,)), ((), ()))
NN = (((1,), (0,)), ((), ()))


def split3(x):
    hi = x.astype(jnp.bfloat16)
    rest = x - hi.astype(jnp.float32)
    mid = rest.astype(jnp.bfloat16)
    low = (rest - mid.astype(jnp.float32)).astype(jnp.bfloat16)
    return hi, mid, low


def dot32(a, b, dims):
    return lax.dot_general(a, b, dims, preferred_element_type=jnp.float32)


def kept_blocks(flags_ref, index_ref, blocks):
    def step(b, count):
        index_ref[count] = b
        return count + flags_ref[b]

    lax.fori_loop(0, blocks, step, jnp.int32(0))


def select_kernel(flags_ref, tokens_ref, out_ref, index_ref, tile_ref):
    rows, features = tokens_ref.shape
    blocks = flags_ref.shape[0]
    width = features // blocks
    per_tile = 128 // width
    kept_blocks(flags_ref, index_ref, blocks)
    for i in range(KEEP_BLK):
        b = index_ref[i]
        start = pl.multiple_of((b // per_tile) * 128, 128)
        tile_ref[...] = tokens_ref[:, pl.ds(start, 128)].astype(jnp.float32).T
        inner = pl.multiple_of((b % per_tile) * width, width)
        out_ref[i * width:(i + 1) * width, :] = tile_ref[pl.ds(inner, width), :].astype(jnp.bfloat16)
    total = jnp.zeros((rows, 128), jnp.float32)
    for c in range(features // 128):
        piece = tokens_ref[:, c * 128:(c + 1) * 128].astype(jnp.float32)
        total += piece * piece
    squares = jnp.sum(total)
    hi, mid, low = split3(jnp.full((EXTRA, rows), squares, jnp.float32))
    row = lax.broadcasted_iota(jnp.int32, (EXTRA, rows), 0)
    zero = jnp.zeros((EXTRA, rows), jnp.float32)
    carried = jnp.where(
        row == 0,
        hi.astype(jnp.float32),
        jnp.where(row == 1, mid.astype(jnp.float32), jnp.where(row == 2, low.astype(jnp.float32), zero)),
    )
    out_ref[KEEP_BLK * width:, :] = carried.astype(jnp.bfloat16)


def select_kept(tokens, keep_flags):
    rows, features = tokens.shape
    blocks = keep_flags.shape[0]
    width = features // blocks
    kept = KEEP_BLK * width
    return pl.pallas_call(
        select_kernel,
        out_shape=jax.ShapeDtypeStruct((kept + EXTRA, rows), jnp.bfloat16),
        in_specs=[
            pl.BlockSpec(memory_space=pltpu.SMEM),
            pl.BlockSpec(memory_space=pltpu.VMEM),
        ],
        out_specs=pl.BlockSpec(memory_space=pltpu.VMEM),
        scratch_shapes=[
            pltpu.SMEM((blocks + 1,), jnp.int32),
            pltpu.VMEM((128, rows), jnp.float32),
        ],
        compiler_params=pltpu.CompilerParams(vmem_limit_bytes=VMEM_LIMIT),
        name="select_kept",
    )(keep_flags, tokens)


def reciprocal(x):
    r = pl.reciprocal(x, approx=True)
    r = r * (2.0 - x * r)
    return r * (2.0 - x * r)


def lane_column(x, c):
    return jnp.broadcast_to(x[:, c:c + 1], (SUB, 128))


def sublane_row(x, t):
    return jnp.broadcast_to(x[t:t + 1, :], (SUB, 128))


def invert_small(cols, sub):
    cols = list(cols)
    for t in range(SUB):
        r = reciprocal(sublane_row(cols[t], t))
        pivot_col = cols[t]
        here = sub == t
        for j in range(SUB):
            if j != t:
                w = sublane_row(cols[j], t) * r
                cols[j] = jnp.where(here, w, cols[j] - pivot_col * w)
        cols[t] = jnp.where(here, r, -(pivot_col * r))
    return cols


def invert_panel(block):
    size = block.shape[0]
    count = size // SUB
    sub = lax.broadcasted_iota(jnp.int32, (SUB, 128), 0)
    lane = lax.broadcasted_iota(jnp.int32, (SUB, 128), 1)
    rows = [block[i * SUB:(i + 1) * SUB, :] for i in range(count)]
    for s in range(count):
        base = s * SUB
        inside = (lane >= base) & (lane < base + SUB)
        cols = invert_small([lane_column(rows[s], base + j) for j in range(SUB)], sub)
        unit = jnp.where(lane == sub + base, 1.0, 0.0)
        pivot_rows = jnp.where(inside, unit, rows[s])
        new = cols[0] * sublane_row(pivot_rows, 0)
        for j in range(1, SUB):
            new = new + cols[j] * sublane_row(pivot_rows, j)
        spread = [sublane_row(new, j) for j in range(SUB)]
        for i in range(count):
            if i != s:
                change = lane_column(rows[i], base) * spread[0]
                for j in range(1, SUB):
                    change = change + lane_column(rows[i], base + j) * spread[j]
                rows[i] = jnp.where(inside, 0.0, rows[i]) - change
        rows[s] = new
    return jnp.concatenate(rows, axis=0)


def wide_left(x):
    hi, mid, low = split3(x)
    return jnp.concatenate([hi, hi, mid, hi, mid, low], axis=1)


def wide_right(x):
    hi, mid, low = split3(x)
    return jnp.concatenate([hi, mid, hi, low, mid, hi], axis=0)


def invert_kernel(*refs):
    pieces = refs[:-5]
    out_ref, damp_ref, all_ref, w_ref, sem = refs[-5:]
    n = len(pieces)
    kept = out_ref.shape[0]
    rows = pieces[0].shape[1]
    copies = [
        pltpu.make_async_copy(pieces[k], all_ref.at[:, k * rows:(k + 1) * rows], sem.at[k]) for k in range(n)
    ]
    for copy in copies:
        copy.start()
    for copy in copies:
        copy.wait()
    features_total = damp_ref[0]
    total = jnp.float32(0.0)
    for k in range(n):
        total = total + jnp.sum(all_ref[kept:, k * rows:k * rows + 1].astype(jnp.float32))
    damping = 0.01 * total / features_total
    spread = jnp.full((8, 128), damping, jnp.float32)
    scale = (1.0 / spread)[0:1, 0:1]
    chunk = 2048 if (n * rows) % 2048 == 0 else rows
    unit = (
        lax.broadcasted_iota(jnp.int32, (kept, PANEL), 0) - lax.broadcasted_iota(jnp.int32, (kept, PANEL), 1)
    )

    @pl.loop(0, kept // PANEL)
    def _(j):
        at = pl.multiple_of(j * PANEL, PANEL)
        acc = jnp.where(unit == at, 1.0, 0.0)
        for c in range(0, n * rows, chunk):
            part = dot32(all_ref[:kept, c:c + chunk], all_ref[pl.ds(at, PANEL), c:c + chunk], NT)
            acc = acc + part * scale
        out_ref[:, pl.ds(at, PANEL)] = acc

    @pl.loop(0, kept // PANEL)
    def _(p):
        at = pl.multiple_of(p * PANEL, PANEL)
        here = pl.ds(at, PANEL)
        inverse = invert_panel(out_ref[here, here])
        w_ref[...] = dot32(wide_left(inverse), wide_right(out_ref[here, :]), NN)
        w_ref[:, here] = inverse
        column = wide_left(out_ref[:, here])
        out_ref[:, here] = jnp.zeros((kept, PANEL), jnp.float32)
        for c in range(0, kept, 256):
            out_ref[:, c:c + 256] -= dot32(column, wide_right(w_ref[:, c:c + 256]), NN)
        out_ref[here, :] = w_ref[...]

    out_ref[...] = out_ref[...] * scale


def invert(pieces, features):
    kept_extra, rows = pieces[0].shape
    kept = kept_extra - EXTRA
    n = len(pieces)
    any_spec = pl.BlockSpec(memory_space=pl.ANY)

    def body(*refs):
        ins, rest = refs[:n], refs[n:]
        invert_kernel(*ins, rest[0], [float(features)], *rest[1:])

    return pl.pallas_call(
        body,
        out_shape=jax.ShapeDtypeStruct((kept, kept), jnp.float32),
        in_specs=[any_spec] * n,
        out_specs=pl.BlockSpec(memory_space=pltpu.VMEM),
        scratch_shapes=[
            pltpu.VMEM((kept_extra, n * rows), jnp.bfloat16),
            pltpu.VMEM((PANEL, kept), jnp.float32),
            pltpu.SemaphoreType.DMA((n,)),
        ],
        compiler_params=pltpu.CompilerParams(vmem_limit_bytes=VMEM_LIMIT),
        name="invert_system",
    )(*pieces)


def apply_kernel(flags_ref, proj_ref, inverse_ref, *refs):
    n = len(refs) - 3
    pieces, (out_ref, index_ref, wide_ref) = refs[:n], refs[n:]
    own, features = out_ref.shape
    blocks = flags_ref.shape[0]
    width = features // blocks
    per_tile = 128 // width
    kept = inverse_ref.shape[0]
    kept_blocks(flags_ref, index_ref, blocks)
    right = jnp.zeros((own, kept), jnp.float32)
    for k in range(n):
        hi, mid, low = split3(proj_ref[k])
        stacked = dot32(jnp.concatenate([hi, mid, low], axis=0), pieces[k][:kept, :], NT)
        right += stacked[:own] + stacked[own:2 * own] + stacked[2 * own:]
    hi, mid, low = split3(right)
    ihi, imid, ilow = split3(inverse_ref[...])
    first = dot32(jnp.concatenate([hi, mid, low], axis=0), ihi, NN)
    second = dot32(jnp.concatenate([hi, mid], axis=0), imid, NN)
    third = dot32(hi, ilow, NN)
    answer = (
        first[:own] + first[own:2 * own] + second[:own] + first[2 * own:] + second[own:] + third
    )
    wide_ref[...] = jnp.zeros((own, features), jnp.float32)
    place = lax.broadcasted_iota(jnp.int32, (own, 128), 1) // width
    for i in range(KEEP_BLK):
        b = index_ref[i]
        start = pl.multiple_of((b // per_tile) * 128, 128)
        inner = b % per_tile
        t = i // per_tile
        source = answer[:, t * 128:(t + 1) * 128]
        moved = pltpu.roll(source, width, 1)
        same = inner == i % per_tile
        value = jnp.where(same, source, moved)
        old = wide_ref[:, pl.ds(start, 128)]
        wide_ref[:, pl.ds(start, 128)] = jnp.where(place == inner, value, old)
    out_ref[...] = wide_ref[...].astype(jnp.bfloat16)


def apply_inverse(keep_flags, projected, inverse, pieces, features):
    n, own, rows = projected.shape
    blocks = keep_flags.shape[0]
    vmem = pl.BlockSpec(memory_space=pltpu.VMEM)
    return pl.pallas_call(
        apply_kernel,
        out_shape=jax.ShapeDtypeStruct((own, features), jnp.bfloat16),
        in_specs=[pl.BlockSpec(memory_space=pltpu.SMEM)] + [vmem] * (2 + n),
        out_specs=vmem,
        scratch_shapes=[
            pltpu.SMEM((blocks + 1,), jnp.int32),
            pltpu.VMEM((own, features), jnp.float32),
        ],
        compiler_params=pltpu.CompilerParams(vmem_limit_bytes=VMEM_LIMIT),
        name="apply_inverse",
    )(keep_flags, projected, inverse, *pieces)


def solution(mesh):
    n = mesh.shape["dp"]

    def swap(x, k):
        return lax.ppermute(x, "dp", [(d, d ^ k) for d in range(n)])

    def on_device(tokens, orig_weight, keep_flags):
        features = tokens.shape[1]
        own = orig_weight.shape[0]
        kept = select_kept(tokens, keep_flags)
        pieces = [None] * n
        pieces[0] = kept
        for k in range(2, n, 2):
            pieces[k] = swap(kept, k)
        for k in range(0, n, 2):
            pieces[k + 1] = swap(pieces[k], 1)
        weights = lax.all_gather(orig_weight, "dp", axis=0, tiled=True)
        projected = lax.dot_general(weights, tokens, NT, preferred_element_type=jnp.float32)
        me = lax.axis_index("dp")
        parts = []
        for k in range(n):
            part = lax.dynamic_slice_in_dim(projected, (me ^ k) * own, own, axis=0)
            parts.append(part if k == 0 else swap(part, k))
        inverse = invert(pieces, features)
        return apply_inverse(keep_flags, jnp.stack(parts), inverse, pieces, features)

    in_specs = (P("dp", None), P(("section", "dp"), None), P())
    out_specs = P(("section", "dp"), None)
    return jax.shard_map(on_device, mesh=mesh, in_specs=in_specs, out_specs=out_specs, check_vma=False)
```

time: 347 us -> 129 us (0.37); the launches traced: 342 us -> 128 us
  other arithmetic: 197 us -> 0 us
  Pallas kernels: 0 us -> 70.8 us
  local copies, waits for them, and re-layouts: 35.9 us -> 0.77 us
  matrix products: 28.1 us -> 2.33 us
  waiting for transfers between devices: 46.8 us -> 29.5 us
  blocking collectives: 16.1 us -> 0 us
  starting transfers between devices: 0.08 us -> 11.5 us
  between operations: 18.5 us -> 13.5 us
    another operation x28 -> x0, other arithmetic: 187 us -> none  [the longest x22 124 us: on_device(): factor = jnp.linalg.cholesky(system)]
    pallas_call x0 -> x3, Pallas kernels: none -> 70.8 us  [the longest x1 60.7 us: invert(): pl.pallas_call(body, out_shape=jax.ShapeDtypeStruct((kept, kept), jnp.flo...]
    psum x1 -> x0, waiting for transfers between devices: 46 us -> none  [on_device(): gramian, total_squares = lax.psum((partial_value, squares), 'dp')]
    ppermute x0 -> x14, waiting for transfers between devices: none -> 28.8 us  [swap(): return lax.ppermute(x, 'dp', [(d, d ^ k) for d in range(n)])]
    another operation x32 -> x0, matrix products: 21.4 us -> none  [the longest x10 12 us: on_device(): factor = jnp.linalg.cholesky(system)]
    another operation x54 -> x1, local copies, waits for them, and re-layouts: 18.1 us -> 0.01 us  [on_device(): jnp.stack(parts)]
    psum x1 -> x0, blocking collectives: 16.1 us -> none  [on_device(): gramian, total_squares = lax.psum((partial_value, squares), 'dp')]
    ppermute x0 -> x14, starting transfers between devices: none -> 11.5 us  [swap(): return lax.ppermute(x, 'dp', [(d, d ^ k) for d in range(n)])]
  transfers between devices with their start and end apart: 3 -> 15, of which waited for: 1 -> 7; matrix products, arithmetic and copies ran while one was open for 66% -> 0% of each run, Pallas kernels for 0% -> 50%
where the time goes in v1:
time: 129 us; the launch traced here: 128 us
  Pallas kernels  70.8 us (55%)
  waiting for transfers between devices  29.5 us (23%)
  between operations  13.5 us (10%)
  starting transfers between devices  11.5 us (9%)
  matrix products  2.33 us (2%)
    pallas_call x1, Pallas kernels, invert(): pl.pallas_call(body, out_shape=jax.ShapeDtypeStruct((kept, kept), jnp.flo...  60.7 us
    ppermute x14, waiting for transfers between devices, swap(): return lax.ppermute(x, 'dp', [(d, d ^ k) for d in range(n)])  28.8 us
    ppermute x14, starting transfers between devices, swap(): return lax.ppermute(x, 'dp', [(d, d ^ k) for d in range(n)])  11.5 us
    pallas_call x1, Pallas kernels, apply_inverse(): pl.pallas_call(apply_kernel, out_shape=jax.ShapeDtypeStruct((own, feature...  6.3 us
    pallas_call x1, Pallas kernels, select_kept(): pl.pallas_call(select_kernel, out_shape=jax.ShapeDtypeStruct((kept + EXTR...  3.75 us
  transfers between devices with their start and end apart: 15, of which 7 were waited for; matrix products, arithmetic and copies ran while one was open for 0% of the time, Pallas kernels for 50%

profile of v1, /device:TPU:0, one launch (start us, length us, event | category | flops | bytes accessed | tf_op | source)
XLA Modules:
  0.0 128.4 jit_solution(5856989782272613837)
XLA Ops:
  6.5 0.0 all-gather.2.cloned.1.call-start
  6.5 0.7 all-gather.2.cloned.1.call-update
  7.3 3.7 %select_kept.1.refs_0_ = bf16[784,256]{1,0:T(8,128)(2,1)} custom-call(s32[64]{0:T(128)} %flags_ref.3, bf16[256,4096]{1,0:T(8,128)(2,1)} %tokens_ref.1), custom_call_target="tpu_custom_call" | custom-call | tf_op jit(solution)/shard_map/select_kept/pallas_call | solution.py:70
  11.0 3.9 %collective-permute-start.12 = (bf16[784,256]{1,0:T(8,128)(2,1)}, bf16[784,256]{1,0:T(8,128)(2,1)S(1)}, u32[]{:S(2)}, u32[]{:S(2)}) collective-permute-start(bf16[784,256]{1,0:T(8,128)(2,1)} %select_kept.1.refs_0_), channel_id=1, source_target_pairs={{0,6},{1,7},{2,4},{3,5},{4,2},{5,3},{6,0},{7,1},{8,14},{9,15},{10,... | collective-permute-start | bytes 1204232 | tf_op jit(solution)/shard_map/ppermute | solution.py:286
  14.9 0.5 collective-permute-start.10
  15.4 0.1 collective-permute-start.8
  15.5 0.0 collective-permute-start.7
  15.5 12.3 %collective-permute-done.12.refs_6_ = bf16[784,256]{1,0:T(8,128)(2,1)S(1)} collective-permute-done((bf16[784,256]{1,0:T(8,128)(2,1)}, bf16[784,256]{1,0:T(8,128)(2,1)S(1)}, u32[]{:S(2)}, u32[]{:S(2)}) %collective-permute-start.12) | collective-permute-done | bytes 401440 | tf_op jit(solution)/shard_map/ppermute | solution.py:286
  27.7 0.0 copy-start.1
  27.7 0.0 collective-permute-start.13
  27.7 8.1 %collective-permute-done.10.refs_4_ = bf16[784,256]{1,0:T(8,128)(2,1)S(1)} collective-permute-done((bf16[784,256]{1,0:T(8,128)(2,1)}, bf16[784,256]{1,0:T(8,128)(2,1)S(1)}, u32[]{:S(2)}, u32[]{:S(2)}) %collective-permute-start.10) | collective-permute-done | bytes 401440 | tf_op jit(solution)/shard_map/ppermute | solution.py:286
  35.8 0.0 copy-start.2
  35.8 0.0 collective-permute-start.11
  35.8 0.3 collective-permute-done.8.refs_2_
  36.1 0.0 copy-start.3
  36.1 0.2 collective-permute-start.9
  36.3 0.0 copy-start
  36.3 0.0 collective-permute-done.7.refs_1_
  36.3 0.0 collective-permute-done.13.refs_7_
  36.3 1.3 %collective-permute-done.11.refs_5_ = bf16[784,256]{1,0:T(8,128)(2,1)} collective-permute-done((bf16[784,256]{1,0:T(8,128)(2,1)S(1)}, bf16[784,256]{1,0:T(8,128)(2,1)}, u32[]{:S(2)}, u32[]{:S(2)}) %collective-permute-start.11) | collective-permute-done | bytes 401440 | tf_op jit(solution)/shard_map/ppermute | solution.py:286
  37.7 1.1 collective-permute-done.9.refs_3_
  38.8 0.0 copy-done.1
  38.8 0.0 copy-done.2
  38.8 0.0 copy-done.3
  38.8 60.7 %invert_system.1.inverse_ref = f32[768,768]{1,0:T(8,128)} custom-call(bf16[784,256]{1,0:T(8,128)(2,1)} %select_kept.1.refs_0_, bf16[784,256]{1,0:T(8,128)(2,1)} %collective-permute-done.7.refs_1_, bf16[784,256]{1,0:T(8,128)(2,1)} %copy-done.3, bf16[784,256]{1,0:T(8,128)(2,1)} %collective-permute-done.9.refs_3_, bf16[784,256]{1,0:T(8,128)(2,1)} %copy-done.2, ...), custom_call_target="tpu_custom_call" | custom-call | tf_op jit(solution)/shard_map/invert_system/pallas_call | solution.py:211
  99.5 0.0 all-gather.2.cloned.1.call-done
  99.6 0.0 copy-done
  99.6 2.3 %fusion = f32[256,256]{1,0:T(8,128)S(1)} fusion(bf16[256,4096]{1,0:T(8,128)(2,1)} %all-gather.2.cloned.1.call-done, bf16[256,4096]{1,0:T(8,128)(2,1)S(1)} %copy-done), kind=kOutput, calls=%fused_computation.15 | convolution fusion | flops 536870912 | bytes 4456448 | tf_op jit(solution)/shard_map/dot_general | solution.py:299
  102.0 0.2 collective-permute-start
  102.2 1.2 collective-permute-start.6
  103.3 1.7 %collective-permute-start.5 = (f32[32,256]{1,0:T(8,128)S(1)}, f32[32,256]{1,0:T(8,128)S(1)}, u32[]{:S(2)}, u32[]{:S(2)}) collective-permute-start(f32[32,256]{1,0:T(8,128)S(1)} %get-tuple-element.6), channel_id=1, source_target_pairs={{0,6},{1,7},{2,4},{3,5},{4,2},{5,3},{6,0},{7,1},{8,14},{9,15},{10,... | collective-permute-start | bytes 98312 | tf_op jit(solution)/shard_map/ppermute | solution.py:286
  105.1 1.2 collective-permute-start.4
  106.3 0.6 collective-permute-start.3
  106.8 0.0 collective-permute-done
  106.9 1.4 %collective-permute-start.1 = (f32[32,256]{1,0:T(8,128)S(1)}, f32[32,256]{1,0:T(8,128)S(1)}, u32[]{:S(2)}, u32[]{:S(2)}) collective-permute-start(f32[32,256]{1,0:T(8,128)S(1)} %get-tuple-element.10), channel_id=1, source_target_pairs={{0,2},{1,3},{2,0},{3,1},{4,6},{5,7},{6,4},{7,5},{8,10},{9,11},{10,... | collective-permute-start | bytes 98312 | tf_op jit(solution)/shard_map/ppermute | solution.py:286
  108.3 2.5 %collective-permute-done.1 = f32[32,256]{1,0:T(8,128)S(1)} collective-permute-done((f32[32,256]{1,0:T(8,128)S(1)}, f32[32,256]{1,0:T(8,128)S(1)}, u32[]{:S(2)}, u32[]{:S(2)}) %collective-permute-start.1) | collective-permute-done | bytes 32800 | tf_op jit(solution)/shard_map/ppermute | solution.py:286
  110.8 0.5 collective-permute-start.2
  111.2 3.2 %collective-permute-done.2 = f32[32,256]{1,0:T(8,128)S(1)} collective-permute-done((f32[32,256]{1,0:T(8,128)S(1)}, f32[32,256]{1,0:T(8,128)S(1)}, u32[]{:S(2)}, u32[]{:S(2)}) %collective-permute-start.2) | collective-permute-done | bytes 32800 | tf_op jit(solution)/shard_map/ppermute | solution.py:286
  114.4 0.0 collective-permute-done.3
  114.4 0.0 collective-permute-done.4
  114.5 0.0 collective-permute-done.5
  114.5 0.0 collective-permute-done.6
  114.5 0.0 copy-start.4
  114.5 0.7 copy-done.4
  115.2 6.3 %apply_inverse.1 = bf16[32,4096]{1,0:T(8,128)(2,1)} custom-call(s32[64]{0:T(128)} %flags_ref.3, f32[8,32,256]{2,1,0:T(8,128)} %copy-done.4, f32[768,768]{1,0:T(8,128)} %invert_system.1.inverse_ref, bf16[784,256]{1,0:T(8,128)(2,1)} %select_kept.1.refs_0_, bf16[784,256]{1,0:T(8,128)(2,1)} %collective-permute-done.7.refs_1_, bf16[784,256]{1,0:T(8,128)(2,1)} %copy-done.3, ...), custom_call_target="tpu_custom_call" | custom-call | tf_op jit(solution)/shard_map/apply_inverse/pallas_call | solution.py:268
  (9 shorter events, 0.1 us)
Async XLA Ops:
  6.5 93.0 %all-gather.2.cloned.1.call-start = ((), (), s32[]{:S(2)}) async-start(), calls=%async_computation | async-start | bytes 2359296 | tf_op jit(solution)/shard_map/all_gather | solution.py:298
  11.0 16.7 %collective-permute-start.12 = (bf16[784,256]{1,0:T(8,128)(2,1)}, bf16[784,256]{1,0:T(8,128)(2,1)S(1)}, u32[]{:S(2)}, u32[]{:S(2)}) collective-permute-start(bf16[784,256]{1,0:T(8,128)(2,1)} %select_kept.1.refs_0_), channel_id=1, source_target_pairs={{0,6},{1,7},{2,4},{3,5},{4,2},{5,3},{6,0},{7,1},{8,14},{9,15},{10,... | collective-permute-start | bytes 1204232 | tf_op jit(solution)/shard_map/ppermute | solution.py:286
  14.9 20.9 %collective-permute-start.10 = (bf16[784,256]{1,0:T(8,128)(2,1)}, bf16[784,256]{1,0:T(8,128)(2,1)S(1)}, u32[]{:S(2)}, u32[]{:S(2)}) collective-permute-start(bf16[784,256]{1,0:T(8,128)(2,1)} %select_kept.1.refs_0_), channel_id=1, source_target_pairs={{0,4},{1,5},{2,6},{3,7},{4,0},{5,1},{6,2},{7,3},{8,12},{9,13},{10,... | collective-permute-start | bytes 1204232 | tf_op jit(solution)/shard_map/ppermute | solution.py:286
  15.4 20.7 %collective-permute-start.8 = (bf16[784,256]{1,0:T(8,128)(2,1)}, bf16[784,256]{1,0:T(8,128)(2,1)S(1)}, u32[]{:S(2)}, u32[]{:S(2)}) collective-permute-start(bf16[784,256]{1,0:T(8,128)(2,1)} %select_kept.1.refs_0_), channel_id=1, source_target_pairs={{0,2},{1,3},{2,0},{3,1},{4,6},{5,7},{6,4},{7,5},{8,10},{9,11},{10,... | collective-permute-start | bytes 1204232 | tf_op jit(solution)/shard_map/ppermute | solution.py:286
  15.5 20.9 %collective-permute-start.7 = (bf16[784,256]{1,0:T(8,128)(2,1)}, bf16[784,256]{1,0:T(8,128)(2,1)}, u32[]{:S(2)}, u32[]{:S(2)}) collective-permute-start(bf16[784,256]{1,0:T(8,128)(2,1)} %select_kept.1.refs_0_), channel_id=1, source_target_pairs={{0,1},{1,0},{2,3},{3,2},{4,5},{5,4},{6,7},{7,6},{8,9},{9,8},{10,11... | collective-permute-start | bytes 1204232 | tf_op jit(solution)/shard_map/ppermute | solution.py:286
  27.7 11.1 %copy-start.1 = (bf16[784,256]{1,0:T(8,128)(2,1)}, bf16[784,256]{1,0:T(8,128)(2,1)S(1)}, u32[]{:S(2)}) copy-start(bf16[784,256]{1,0:T(8,128)(2,1)S(1)} %collective-permute-done.12.refs_6_) | copy-start | bytes 1204228
  27.7 8.6 %collective-permute-start.13 = (bf16[784,256]{1,0:T(8,128)(2,1)S(1)}, bf16[784,256]{1,0:T(8,128)(2,1)}, u32[]{:S(2)}, u32[]{:S(2)}) collective-permute-start(bf16[784,256]{1,0:T(8,128)(2,1)S(1)} %collective-permute-done.12.refs_6_), channel_id=1, source_target_pairs={{0,1},{1,0},{2,3},{3,2},{4,5},{5,4},{6,7},{7,6},{8,9},{9,8},{10,11... | collective-permute-start | bytes 1204232 | tf_op jit(solution)/shard_map/ppermute | solution.py:286
  35.8 3.0 %copy-start.2 = (bf16[784,256]{1,0:T(8,128)(2,1)}, bf16[784,256]{1,0:T(8,128)(2,1)S(1)}, u32[]{:S(2)}) copy-start(bf16[784,256]{1,0:T(8,128)(2,1)S(1)} %collective-permute-done.10.refs_4_) | copy-start | bytes 1204228
  35.8 1.9 %collective-permute-start.11 = (bf16[784,256]{1,0:T(8,128)(2,1)S(1)}, bf16[784,256]{1,0:T(8,128)(2,1)}, u32[]{:S(2)}, u32[]{:S(2)}) collective-permute-start(bf16[784,256]{1,0:T(8,128)(2,1)S(1)} %collective-permute-done.10.refs_4_), channel_id=1, source_target_pairs={{0,1},{1,0},{2,3},{3,2},{4,5},{5,4},{6,7},{7,6},{8,9},{9,8},{10,11... | collective-permute-start | bytes 1204232 | tf_op jit(solution)/shard_map/ppermute | solution.py:286
  36.1 2.7 %copy-start.3 = (bf16[784,256]{1,0:T(8,128)(2,1)}, bf16[784,256]{1,0:T(8,128)(2,1)S(1)}, u32[]{:S(2)}) copy-start(bf16[784,256]{1,0:T(8,128)(2,1)S(1)} %collective-permute-done.8.refs_2_) | copy-start | bytes 1204228
  36.1 2.7 %collective-permute-start.9 = (bf16[784,256]{1,0:T(8,128)(2,1)S(1)}, bf16[784,256]{1,0:T(8,128)(2,1)}, u32[]{:S(2)}, u32[]{:S(2)}) collective-permute-start(bf16[784,256]{1,0:T(8,128)(2,1)S(1)} %collective-permute-done.8.refs_2_), channel_id=1, source_target_pairs={{0,1},{1,0},{2,3},{3,2},{4,5},{5,4},{6,7},{7,6},{8,9},{9,8},{10,11... | collective-permute-start | bytes 1204232 | tf_op jit(solution)/shard_map/ppermute | solution.py:286
  36.3 63.3 %copy-start = (bf16[256,4096]{1,0:T(8,128)(2,1)S(1)}, bf16[256,4096]{1,0:T(8,128)(2,1)}, u32[]{:S(2)}) copy-start(bf16[256,4096]{1,0:T(8,128)(2,1)} %tokens_ref.1) | copy-start | bytes 6291460
  102.0 4.9 %collective-permute-start = (f32[32,256]{1,0:T(8,128)S(1)}, f32[32,256]{1,0:T(8,128)S(1)}, u32[]{:S(2)}, u32[]{:S(2)}) collective-permute-start(f32[32,256]{1,0:T(8,128)S(1)} %get-tuple-element.11), channel_id=1, source_target_pairs={{0,1},{1,0},{2,3},{3,2},{4,5},{5,4},{6,7},{7,6},{8,9},{9,8},{10,11... | collective-permute-start | bytes 98312 | tf_op jit(solution)/shard_map/ppermute | solution.py:286
  102.2 12.3 %collective-permute-start.6 = (f32[32,256]{1,0:T(8,128)S(1)}, f32[32,256]{1,0:T(8,128)S(1)}, u32[]{:S(2)}, u32[]{:S(2)}) collective-permute-start(f32[32,256]{1,0:T(8,128)S(1)} %get-tuple-element.5), channel_id=1, source_target_pairs={{0,7},{1,6},{2,5},{3,4},{4,3},{5,2},{6,1},{7,0},{8,15},{9,14},{10,... | collective-permute-start | bytes 98312 | tf_op jit(solution)/shard_map/ppermute | solution.py:286
  103.3 11.1 %collective-permute-start.5 = (f32[32,256]{1,0:T(8,128)S(1)}, f32[32,256]{1,0:T(8,128)S(1)}, u32[]{:S(2)}, u32[]{:S(2)}) collective-permute-start(f32[32,256]{1,0:T(8,128)S(1)} %get-tuple-element.6), channel_id=1, source_target_pairs={{0,6},{1,7},{2,4},{3,5},{4,2},{5,3},{6,0},{7,1},{8,14},{9,15},{10,... | collective-permute-start | bytes 98312 | tf_op jit(solution)/shard_map/ppermute | solution.py:286
  105.1 9.4 %collective-permute-start.4 = (f32[32,256]{1,0:T(8,128)S(1)}, f32[32,256]{1,0:T(8,128)S(1)}, u32[]{:S(2)}, u32[]{:S(2)}) collective-permute-start(f32[32,256]{1,0:T(8,128)S(1)} %get-tuple-element.7), channel_id=1, source_target_pairs={{0,5},{1,4},{2,7},{3,6},{4,1},{5,0},{6,3},{7,2},{8,13},{9,12},{10,... | collective-permute-start | bytes 98312 | tf_op jit(solution)/shard_map/ppermute | solution.py:286
  106.3 8.1 %collective-permute-start.3 = (f32[32,256]{1,0:T(8,128)S(1)}, f32[32,256]{1,0:T(8,128)S(1)}, u32[]{:S(2)}, u32[]{:S(2)}) collective-permute-start(f32[32,256]{1,0:T(8,128)S(1)} %get-tuple-element.8), channel_id=1, source_target_pairs={{0,4},{1,5},{2,6},{3,7},{4,0},{5,1},{6,2},{7,3},{8,12},{9,13},{10,... | collective-permute-start | bytes 98312 | tf_op jit(solution)/shard_map/ppermute | solution.py:286
  106.9 3.9 %collective-permute-start.1 = (f32[32,256]{1,0:T(8,128)S(1)}, f32[32,256]{1,0:T(8,128)S(1)}, u32[]{:S(2)}, u32[]{:S(2)}) collective-permute-start(f32[32,256]{1,0:T(8,128)S(1)} %get-tuple-element.10), channel_id=1, source_target_pairs={{0,2},{1,3},{2,0},{3,1},{4,6},{5,7},{6,4},{7,5},{8,10},{9,11},{10,... | collective-permute-start | bytes 98312 | tf_op jit(solution)/shard_map/ppermute | solution.py:286
  110.8 3.7 %collective-permute-start.2 = (f32[32,256]{1,0:T(8,128)S(1)}, f32[32,256]{1,0:T(8,128)S(1)}, u32[]{:S(2)}, u32[]{:S(2)}) collective-permute-start(f32[32,256]{1,0:T(8,128)S(1)} %get-tuple-element.9), channel_id=1, source_target_pairs={{0,3},{1,2},{2,1},{3,0},{4,7},{5,6},{6,5},{7,4},{8,11},{9,10},{10,... | collective-permute-start | bytes 98312 | tf_op jit(solution)/shard_map/ppermute | solution.py:286
  114.5 0.7 copy-start.4
Sparse Core Ops, SparseCore 0:
  9.2 37.1 all-gather.1

commit v2 on v1

v2 whole, which is shorter than its diff:
```python
import functools

import jax
import jax.numpy as jnp
from jax import lax
from jax.experimental import pallas as pl
from jax.experimental.pallas import tpu as pltpu
from jax.sharding import PartitionSpec as P

KEEP_BLK = 12
PANEL = 128
SUB = 8
EXTRA = 16
VMEM_LIMIT = 56 * 1024 * 1024
NT = (((1,), (1,)), ((), ()))
NN = (((1,), (0,)), ((), ()))


def split3(x):
    hi = x.astype(jnp.bfloat16)
    rest = x - hi.astype(jnp.float32)
    mid = rest.astype(jnp.bfloat16)
    low = (rest - mid.astype(jnp.float32)).astype(jnp.bfloat16)
    return hi, mid, low


def dot32(a, b, dims):
    return lax.dot_general(a, b, dims, preferred_element_type=jnp.float32)


def kept_blocks(flags_ref, index_ref):
    count = jnp.int32(0)
    for b in range(flags_ref.shape[0]):
        index_ref[count] = b
        count = count + flags_ref[b]


def select_kernel(flags_ref, tokens_ref, out_ref, index_ref, tile_ref, chunk_ref, tile_sem, chunk_sem):
    rows, features = tokens_ref.shape
    blocks = flags_ref.shape[0]
    width = features // blocks
    per_tile = 128 // width
    chunks = chunk_ref.shape[0]
    step = rows // chunks
    kept_blocks(flags_ref, index_ref)
    tiles = []
    for i in range(KEEP_BLK):
        start = pl.multiple_of((index_ref[i] // per_tile) * 128, 128)
        tiles.append(
            pltpu.make_async_copy(tokens_ref.at[:, pl.ds(start, 128)], tile_ref.at[i], tile_sem.at[i])
        )
        tiles[-1].start()
    reads = []
    for c in range(chunks):
        reads.append(
            pltpu.make_async_copy(tokens_ref.at[c * step:(c + 1) * step, :], chunk_ref.at[c], chunk_sem.at[c])
        )
        reads[-1].start()
    row = lax.broadcasted_iota(jnp.int32, (width, 128), 0)
    lane = lax.broadcasted_iota(jnp.int32, (width, 128), 1)
    for i in range(KEEP_BLK):
        inner = (index_ref[i] % per_tile) * width
        pick = jnp.where(lane == row + inner, 1.0, 0.0).astype(jnp.bfloat16)
        tiles[i].wait()
        out_ref[i * width:(i + 1) * width, :] = dot32(pick, tile_ref[i], NT).astype(jnp.bfloat16)
    total = jnp.zeros((step, 128), jnp.float32)
    for c in range(chunks):
        reads[c].wait()
        for f in range(features // 128):
            piece = chunk_ref[c, :, f * 128:(f + 1) * 128].astype(jnp.float32)
            total += piece * piece
    squares = jnp.sum(total)
    hi, mid, low = split3(jnp.full((EXTRA, rows), squares, jnp.float32))
    row = lax.broadcasted_iota(jnp.int32, (EXTRA, rows), 0)
    carried = jnp.where(
        row == 0,
        hi.astype(jnp.float32),
        jnp.where(row == 1, mid.astype(jnp.float32), jnp.where(row == 2, low.astype(jnp.float32), 0.0)),
    )
    out_ref[KEEP_BLK * width:, :] = carried.astype(jnp.bfloat16)


def select_kept(tokens, keep_flags):
    rows, features = tokens.shape
    blocks = keep_flags.shape[0]
    kept = KEEP_BLK * (features // blocks)
    chunks = 4
    return pl.pallas_call(
        select_kernel,
        out_shape=jax.ShapeDtypeStruct((kept + EXTRA, rows), jnp.bfloat16),
        in_specs=[
            pl.BlockSpec(memory_space=pltpu.SMEM),
            pl.BlockSpec(memory_space=pl.ANY),
        ],
        out_specs=pl.BlockSpec(memory_space=pltpu.VMEM),
        scratch_shapes=[
            pltpu.SMEM((blocks + 1,), jnp.int32),
            pltpu.VMEM((KEEP_BLK, rows, 128), jnp.bfloat16),
            pltpu.VMEM((chunks, rows // chunks, features), jnp.bfloat16),
            pltpu.SemaphoreType.DMA((KEEP_BLK,)),
            pltpu.SemaphoreType.DMA((chunks,)),
        ],
        compiler_params=pltpu.CompilerParams(vmem_limit_bytes=VMEM_LIMIT),
        name="select_kept",
    )(keep_flags, tokens)


def lane_column(x, c):
    return jnp.broadcast_to(x[:, c:c + 1], (SUB, 128))


def sublane_row(x, t):
    return jnp.broadcast_to(x[t:t + 1, :], (SUB, 128))


def tree_sum(terms):
    while len(terms) > 1:
        pairs = [terms[i] + terms[i + 1] for i in range(0, len(terms) - 1, 2)]
        terms = pairs + terms[len(terms) - len(terms) % 2:]
    return terms[0]


def invert_small(cols, sub):
    cols = list(cols)
    r = pl.reciprocal(sublane_row(cols[0], 0), approx=True)
    for t in range(SUB):
        here = sub == t
        after = None
        if t + 1 < SUB:
            product = sublane_row(cols[t + 1], t) * sublane_row(cols[t], t + 1)
            after = pl.reciprocal(sublane_row(cols[t + 1], t + 1) - product * r, approx=True)
        pivot_col = jnp.where(here, -1.0, cols[t])
        for j in range(SUB):
            if j != t:
                w = sublane_row(cols[j], t) * r
                cols[j] = jnp.where(here, 0.0, cols[j]) - pivot_col * w
        cols[t] = -(pivot_col * r)
        r = after
    return cols


def invert_panel(block):
    size = block.shape[0]
    count = size // SUB
    sub = lax.broadcasted_iota(jnp.int32, (SUB, 128), 0)
    lane = lax.broadcasted_iota(jnp.int32, (SUB, 128), 1)
    rows = [block[i * SUB:(i + 1) * SUB, :] for i in range(count)]
    for s in range(count):
        base = s * SUB
        inside = (lane >= base) & (lane < base + SUB)
        cols = invert_small([lane_column(rows[s], base + j) for j in range(SUB)], sub)
        pivot_rows = jnp.where(inside, jnp.where(lane == sub + base, 1.0, 0.0), rows[s])
        new = tree_sum([cols[j] * sublane_row(pivot_rows, j) for j in range(SUB)])
        spread = [sublane_row(new, j) for j in range(SUB)]
        for i in [(s + d) % count for d in range(1, count)]:
            change = tree_sum([lane_column(rows[i], base + j) * spread[j] for j in range(SUB)])
            rows[i] = jnp.where(inside, 0.0, rows[i]) - change
        rows[s] = new
    return jnp.concatenate(rows, axis=0)


def wide_left(x):
    hi, mid, low = split3(x)
    return jnp.concatenate([hi, hi, mid, hi, mid, low], axis=1)


def wide_right(x):
    hi, mid, low = split3(x)
    return jnp.concatenate([hi, mid, hi, low, mid, hi], axis=0)


def sweep(first, last, a_ref, left_ref, right_ref, scale=None):
    kept = a_ref.shape[0]
    left_ref[...] = jnp.zeros_like(left_ref)
    right_ref[...] = jnp.zeros_like(right_ref)
    row = lax.broadcasted_iota(jnp.int32, (kept, PANEL), 0)

    @pl.loop(first, last)
    def _(p):
        at = pl.multiple_of(p * PANEL, PANEL)
        here = pl.ds(at, PANEL)
        inverse = invert_panel(a_ref[here, here] - dot32(left_ref[here, :], right_ref[:, here], NN))
        for c in range(0, kept, 256):
            a_ref[:, c:c + 256] -= dot32(left_ref[...], right_ref[:, c:c + 256], NN)
        column = jnp.where((row >= at) & (row < at + PANEL), 0.0, a_ref[:, here])
        left_ref[...] = wide_left(column)
        a_ref[:, here] = jnp.zeros((kept, PANEL), jnp.float32)
        wide = wide_left(inverse)
        for c in range(0, kept, 256):
            a_ref[here, c:c + 256] = dot32(wide, wide_right(a_ref[here, c:c + 256]), NN)
        a_ref[here, here] = inverse
        right_ref[...] = wide_right(a_ref[here, :])

    for c in range(0, kept, 256):
        value = a_ref[:, c:c + 256] - dot32(left_ref[...], right_ref[:, c:c + 256], NN)
        a_ref[:, c:c + 256] = value if scale is None else value * scale


def first_kernel(features, last, *refs):
    pieces = refs[:-6]
    out_ref, scale_ref, all_ref, left_ref, right_ref, sem = refs[-6:]
    n = len(pieces)
    kept = out_ref.shape[0]
    rows = pieces[0].shape[1]
    copies = [
        pltpu.make_async_copy(pieces[k], all_ref.at[:, k * rows:(k + 1) * rows], sem.at[k]) for k in range(n)
    ]
    for copy in copies:
        copy.start()
    for copy in copies:
        copy.wait()
    total = jnp.float32(0.0)
    for k in range(n):
        total = total + jnp.sum(all_ref[kept:, k * rows:k * rows + 1].astype(jnp.float32))
    scale_ref[...] = 1.0 / jnp.full(scale_ref.shape, 0.01 * total / features, jnp.float32)
    scale = scale_ref[0:1, 0:1]
    chunk = 2048 if (n * rows) % 2048 == 0 else rows
    tile = 256
    unit = lax.broadcasted_iota(jnp.int32, (kept, tile), 0) - lax.broadcasted_iota(jnp.int32, (kept, tile), 1)

    @pl.loop(0, kept // tile)
    def _(j):
        at = pl.multiple_of(j * tile, tile)
        acc = jnp.where(unit == at, 1.0, 0.0)
        for c in range(0, n * rows, chunk):
            part = dot32(all_ref[:kept, c:c + chunk], all_ref[pl.ds(at, tile), c:c + chunk], NT)
            acc = acc + part * scale
        out_ref[:, pl.ds(at, tile)] = acc

    sweep(0, last, out_ref, left_ref, right_ref)


def first_half(pieces, features, last):
    kept_extra, rows = pieces[0].shape
    kept = kept_extra - EXTRA
    n = len(pieces)
    return pl.pallas_call(
        functools.partial(first_kernel, float(features), last),
        out_shape=[
            jax.ShapeDtypeStruct((kept, kept), jnp.float32),
            jax.ShapeDtypeStruct((8, 128), jnp.float32),
        ],
        in_specs=[pl.BlockSpec(memory_space=pl.ANY)] * n,
        out_specs=[pl.BlockSpec(memory_space=pltpu.VMEM)] * 2,
        scratch_shapes=[
            pltpu.VMEM((kept_extra, n * rows), jnp.bfloat16),
            pltpu.VMEM((kept, 6 * PANEL), jnp.bfloat16),
            pltpu.VMEM((6 * PANEL, kept), jnp.bfloat16),
            pltpu.SemaphoreType.DMA((n,)),
        ],
        compiler_params=pltpu.CompilerParams(vmem_limit_bytes=VMEM_LIMIT),
        name="gram_and_first_panels",
    )(*pieces)


def second_kernel(first, a_ref, scale_ref, out_ref, left_ref, right_ref):
    kept = out_ref.shape[0]
    out_ref[...] = a_ref[...]
    sweep(first, kept // PANEL, out_ref, left_ref, right_ref, scale_ref[0:1, 0:1])


def second_half(a, scale, first):
    kept = a.shape[0]
    vmem = pl.BlockSpec(memory_space=pltpu.VMEM)
    return pl.pallas_call(
        functools.partial(second_kernel, first),
        out_shape=jax.ShapeDtypeStruct((kept, kept), jnp.float32),
        in_specs=[vmem, vmem],
        out_specs=vmem,
        scratch_shapes=[
            pltpu.VMEM((kept, 6 * PANEL), jnp.bfloat16),
            pltpu.VMEM((6 * PANEL, kept), jnp.bfloat16),
        ],
        compiler_params=pltpu.CompilerParams(vmem_limit_bytes=VMEM_LIMIT),
        name="last_panels",
    )(a, scale)


def apply_kernel(chips, flags_ref, *refs):
    projected, refs = refs[:chips], refs[chips:]
    inverse_ref, refs = refs[0], refs[1:]
    pieces, (out_ref, index_ref, wide_ref) = refs[:2 * chips], refs[2 * chips:]
    own, features = out_ref.shape
    blocks = flags_ref.shape[0]
    width = features // blocks
    per_tile = 128 // width
    kept = inverse_ref.shape[0]
    rows = pieces[0].shape[1]
    kept_blocks(flags_ref, index_ref)
    right = jnp.zeros((3 * own, kept), jnp.float32)
    for k in range(chips):
        for core in range(2):
            hi, mid, low = split3(projected[k][:, core * rows:(core + 1) * rows])
            right += dot32(jnp.concatenate([hi, mid, low], axis=0), pieces[2 * k + core][:kept, :], NT)
    right = right[:own] + right[own:2 * own] + right[2 * own:]
    hi, mid, low = split3(right)
    ihi, imid, ilow = split3(inverse_ref[...])
    first = dot32(jnp.concatenate([hi, mid, low], axis=0), ihi, NN)
    second = dot32(jnp.concatenate([hi, mid], axis=0), imid, NN)
    third = dot32(hi, ilow, NN)
    answer = first[:own] + first[own:2 * own] + second[:own] + first[2 * own:] + second[own:] + third
    wide_ref[...] = jnp.zeros((own, features), jnp.float32)
    place = lax.broadcasted_iota(jnp.int32, (own, 128), 1) // width
    for i in range(KEEP_BLK):
        b = index_ref[i]
        start = pl.multiple_of((b // per_tile) * 128, 128)
        inner = b % per_tile
        t = i // per_tile
        source = answer[:, t * 128:(t + 1) * 128]
        moved = pltpu.roll(source, width, 1)
        value = jnp.where(inner == i % per_tile, source, moved)
        old = wide_ref[:, pl.ds(start, 128)]
        wide_ref[:, pl.ds(start, 128)] = jnp.where(place == inner, value, old)
    out_ref[...] = wide_ref[...].astype(jnp.bfloat16)


def apply_inverse(keep_flags, projected, inverse, pieces, features):
    own = projected[0].shape[0]
    blocks = keep_flags.shape[0]
    chips = len(projected)
    vmem = pl.BlockSpec(memory_space=pltpu.VMEM)
    return pl.pallas_call(
        functools.partial(apply_kernel, chips),
        out_shape=jax.ShapeDtypeStruct((own, features), jnp.bfloat16),
        in_specs=[pl.BlockSpec(memory_space=pltpu.SMEM)] + [vmem] * (1 + 3 * chips),
        out_specs=vmem,
        scratch_shapes=[
            pltpu.SMEM((blocks + 1,), jnp.int32),
            pltpu.VMEM((own, features), jnp.float32),
        ],
        compiler_params=pltpu.CompilerParams(vmem_limit_bytes=VMEM_LIMIT),
        name="apply_inverse",
    )(keep_flags, *projected, inverse, *pieces)


def solution(mesh):
    n = mesh.shape["dp"]
    others = range(2, n, 2)

    def swap(x, k):
        return lax.ppermute(x, "dp", [(d, d ^ k) for d in range(n)])

    def on_device(tokens, orig_weight, keep_flags):
        features = tokens.shape[1]
        own = orig_weight.shape[0]
        kept = select_kept(tokens, keep_flags)
        panels = (kept.shape[0] - EXTRA) // PANEL
        half = panels // 2
        same = [kept] + [swap(kept, k) for k in others]
        pieces = []
        for piece in same:
            pieces += [piece, swap(piece, 1)]
        pieces, orig_weight = lax.optimization_barrier((pieces, orig_weight))
        sibling = swap(tokens, 1)
        weights = [orig_weight] + [swap(orig_weight, k) for k in others]
        begun, scale = first_half(pieces, features, half)
        begun, weights, sibling = lax.optimization_barrier((begun, weights, sibling))
        stacked = jnp.concatenate(weights, axis=0)
        projected = [
            lax.dot_general(stacked, part, NT, preferred_element_type=jnp.float32) for part in (tokens, sibling)
        ]
        projected = jnp.concatenate(projected, axis=1)
        begun, projected = lax.optimization_barrier((begun, projected))
        parts = [projected[i * own:(i + 1) * own] for i in range(n // 2)]
        parts = [parts[0]] + [swap(part, k) for part, k in zip(parts[1:], others)]
        inverse = second_half(begun, scale, half)
        return apply_inverse(keep_flags, parts, inverse, pieces, features)

    in_specs = (P("dp", None), P(("section", "dp"), None), P())
    out_specs = P(("section", "dp"), None)
    return jax.shard_map(on_device, mesh=mesh, in_specs=in_specs, out_specs=out_specs, check_vma=False)
```

time: 129 us -> 91.8 us (0.71)
  Pallas kernels: 70.8 us -> 56.3 us
  between operations: 13.5 us -> 0.2 us
  waiting for transfers between devices: 29.5 us -> 20 us
    pallas_call x2 -> x3, Pallas kernels: 67 us -> 51.3 us  [the longest x1 24.2 us: first_half(): pl.pallas_call(functools.partial(first_kernel, float(features), last), ou...]
    ppermute x14, waiting for transfers between devices: 28.8 us -> 20 us  [swap(): return lax.ppermute(x, 'dp', [(d, d ^ k) for d in range(n)])]
  transfers between devices with their start and end apart: 15 -> 14, of which waited for: 7 -> 5; matrix products, arithmetic and copies ran while one was open for 0% -> 0% of each run, Pallas kernels for 50% -> 55%
where the time goes in v2:
time: 91.8 us; the launch traced here: 91.6 us
  Pallas kernels  56.3 us (61%)
  waiting for transfers between devices  20 us (22%)
  starting transfers between devices  12 us (13%)
  matrix products  1.67 us (2%)
  local copies, waits for them, and re-layouts  1.39 us (2%)
    pallas_call x1, Pallas kernels, first_half(): pl.pallas_call(functools.partial(first_kernel, float(features), last), ou...  24.2 us
    pallas_call x1, Pallas kernels, second_half(): pl.pallas_call(functools.partial(second_kernel, first), out_shape=jax.Sha...  21.1 us
    ppermute x14, waiting for transfers between devices, swap(): return lax.ppermute(x, 'dp', [(d, d ^ k) for d in range(n)])  20 us
    ppermute x14, starting transfers between devices, swap(): return lax.ppermute(x, 'dp', [(d, d ^ k) for d in range(n)])  12 us
    pallas_call x1, Pallas kernels, apply_inverse(): pl.pallas_call(functools.partial(apply_kernel, chips), out_shape=jax.Shap...  5.96 us
    pallas_call x1, Pallas kernels, select_kept(): pl.pallas_call(select_kernel, out_shape=jax.ShapeDtypeStruct((kept + EXTR...  5.01 us
  transfers between devices with their start and end apart: 14, of which 5 were waited for; matrix products, arithmetic and copies ran while one was open for 0% of the time, Pallas kernels for 55%

profile of v2, /device:TPU:0, one launch (start us, length us, event | category | flops | bytes accessed | tf_op | source)
XLA Modules:
  0.0 91.6 jit_solution(14907922540010142405)
XLA Ops:
  0.0 0.0 copy-start.8
  0.0 0.5 collective-permute-start.10
  0.5 5.0 %select_kept.1.refs_0_.refs_5_ = bf16[784,256]{1,0:T(8,128)(2,1)} custom-call(s32[64]{0:T(128)} %flags_ref.3, bf16[256,4096]{1,0:T(8,128)(2,1)} %tokens_ref.1), custom_call_target="tpu_custom_call" | custom-call | tf_op jit(solution)/shard_map/select_kept/pallas_call | solution.py:88
  5.5 0.0 copy-start
  5.5 3.7 %collective-permute-start.5 = (bf16[784,256]{1,0:T(8,128)(2,1)}, bf16[784,256]{1,0:T(8,128)(2,1)S(1)}, u32[]{:S(2)}, u32[]{:S(2)}) collective-permute-start(bf16[784,256]{1,0:T(8,128)(2,1)} %select_kept.1.refs_0_.refs_5_), channel_id=1, source_target_pairs={{0,6},{1,7},{2,4},{3,5},{4,2},{5,3},{6,0},{7,1},{8,14},{9,15},{10,... | collective-permute-start | bytes 1204232 | tf_op jit(solution)/shard_map/ppermute | solution.py:341
  9.1 0.5 collective-permute-start.3
  9.6 0.1 collective-permute-start.1
  9.8 0.0 collective-permute-start
  9.8 9.7 %collective-permute-done.5.refs_6_.refs_11_ = bf16[784,256]{1,0:T(8,128)(2,1)S(1)} collective-permute-done((bf16[784,256]{1,0:T(8,128)(2,1)}, bf16[784,256]{1,0:T(8,128)(2,1)S(1)}, u32[]{:S(2)}, u32[]{:S(2)}) %collective-permute-start.5) | collective-permute-done | bytes 401440 | tf_op jit(solution)/shard_map/ppermute | solution.py:341
  19.5 0.0 copy-start.1
  19.5 0.0 collective-permute-start.6
  19.5 8.2 %collective-permute-done.3.refs_4_.refs_9_ = bf16[784,256]{1,0:T(8,128)(2,1)S(1)} collective-permute-done((bf16[784,256]{1,0:T(8,128)(2,1)}, bf16[784,256]{1,0:T(8,128)(2,1)S(1)}, u32[]{:S(2)}, u32[]{:S(2)}) %collective-permute-start.3) | collective-permute-done | bytes 401440 | tf_op jit(solution)/shard_map/ppermute | solution.py:341
  27.8 0.0 copy-start.2
  27.8 0.0 collective-permute-start.4
  27.8 0.3 collective-permute-done.1.refs_2_.refs_7_
  28.1 0.0 copy-start.3
  28.1 0.2 collective-permute-start.2
  28.3 0.0 collective-permute-done.refs_1_.refs_6_
  28.3 0.0 copy-start.4
  28.3 0.0 collective-permute-done.6.refs_7_.refs_12_
  28.3 0.0 copy-start.5
  28.3 1.2 %collective-permute-done.4.refs_5_.refs_10_ = bf16[784,256]{1,0:T(8,128)(2,1)S(1)} collective-permute-done((bf16[784,256]{1,0:T(8,128)(2,1)S(1)}, bf16[784,256]{1,0:T(8,128)(2,1)S(1)}, u32[]{:S(2)}, u32[]{:S(2)}) %collective-permute-start.4) | collective-permute-done | bytes 401440 | tf_op jit(solution)/shard_map/ppermute | solution.py:341
  29.5 0.0 copy-start.6
  29.5 0.6 collective-permute-done.2.refs_3_.refs_8_
  30.1 0.0 copy-done.8
  30.1 0.0 copy-start.7
  30.1 1.8 %collective-permute-start.9 = (bf16[32,4096]{1,0:T(8,128)(2,1)S(1)}, bf16[32,4096]{1,0:T(8,128)(2,1)S(1)}, u32[]{:S(2)}, u32[]{:S(2)}) collective-permute-start(bf16[32,4096]{1,0:T(8,128)(2,1)S(1)} %copy-done.8), channel_id=1, source_target_pairs={{0,6},{1,7},{2,4},{3,5},{4,2},{5,3},{6,0},{7,1},{8,14},{9,15},{10,... | collective-permute-start | bytes 786440 | tf_op jit(solution)/shard_map/ppermute | solution.py:341
  31.9 1.3 %collective-permute-start.8 = (bf16[32,4096]{1,0:T(8,128)(2,1)S(1)}, bf16[32,4096]{1,0:T(8,128)(2,1)S(1)}, u32[]{:S(2)}, u32[]{:S(2)}) collective-permute-start(bf16[32,4096]{1,0:T(8,128)(2,1)S(1)} %copy-done.8), channel_id=1, source_target_pairs={{0,4},{1,5},{2,6},{3,7},{4,0},{5,1},{6,2},{7,3},{8,12},{9,13},{10,... | collective-permute-start | bytes 786440 | tf_op jit(solution)/shard_map/ppermute | solution.py:341
  33.2 0.3 collective-permute-start.7
  33.6 0.0 copy-done.1
  33.6 0.0 copy-done.2
  33.6 0.0 copy-done.3
  33.6 0.0 copy-done.4
  33.6 0.0 copy-done.5
  33.6 0.0 copy-done.6
  33.6 0.0 copy-done.7
  33.6 24.2 %gram_and_first_panels.1 = (f32[768,768]{1,0:T(8,128)}, f32[8,128]{1,0:T(8,128)}) custom-call(bf16[784,256]{1,0:T(8,128)(2,1)} %select_kept.1.refs_0_.refs_5_, bf16[784,256]{1,0:T(8,128)(2,1)} %copy-done.4, bf16[784,256]{1,0:T(8,128)(2,1)} %copy-done.3, bf16[784,256]{1,0:T(8,128)(2,1)} %copy-done.7, bf16[784,256]{1,0:T(8,128)(2,1)} %copy-done.2, ...), custom_call_target="tpu_custom_call" | custom-call | tf_op jit(solution)/shard_map/gram_and_first_panels/pallas_call | solution.py:237
  57.9 0.0 collective-permute-done.9
  57.9 0.0 collective-permute-done.8
  57.9 0.0 collective-permute-done.7
  57.9 0.0 collective-permute-done.10
  58.0 0.0 copy-done
  58.0 0.8 fusion.1
  58.9 0.8 fusion.2
  59.7 0.6 fusion
  60.4 1.8 %collective-permute-start.13 = (f32[32,512]{1,0:T(8,128)S(1)}, f32[32,512]{1,0:T(8,128)S(1)}, u32[]{:S(2)}, u32[]{:S(2)}) collective-permute-start(f32[32,512]{1,0:T(8,128)S(1)} %get-tuple-element.43), channel_id=1, source_target_pairs={{0,6},{1,7},{2,4},{3,5},{4,2},{5,3},{6,0},{7,1},{8,14},{9,15},{10,... | collective-permute-start | bytes 196616 | tf_op jit(solution)/shard_map/ppermute | solution.py:341
  62.2 1.3 %collective-permute-start.12 = (f32[32,512]{1,0:T(8,128)S(1)}, f32[32,512]{1,0:T(8,128)S(1)}, u32[]{:S(2)}, u32[]{:S(2)}) collective-permute-start(f32[32,512]{1,0:T(8,128)S(1)} %get-tuple-element.44), channel_id=1, source_target_pairs={{0,4},{1,5},{2,6},{3,7},{4,0},{5,1},{6,2},{7,3},{8,12},{9,13},{10,... | collective-permute-start | bytes 196616 | tf_op jit(solution)/shard_map/ppermute | solution.py:341
  63.5 0.3 collective-permute-start.11
  63.9 21.1 %last_panels.1.refs_4_ = f32[768,768]{1,0:T(8,128)} custom-call(f32[768,768]{1,0:T(8,128)} %get-tuple-element.41.a_ref, f32[8,128]{1,0:T(8,128)} %get-tuple-element.42.scale_ref), custom_call_target="tpu_custom_call" | custom-call | tf_op jit(solution)/shard_map/last_panels/pallas_call | solution.py:265
  85.0 0.0 collective-permute-done.13.refs_3_
  85.0 0.0 copy-start.9
  85.0 0.0 collective-permute-done.12.refs_2_
  85.0 0.0 copy-start.10
  85.0 0.0 collective-permute-done.11.refs_1_
  85.0 0.0 copy-start.11
  85.0 0.6 copy-done.9
  85.6 0.0 copy-done.10
  85.6 0.0 copy-done.11
  85.7 6.0 %apply_inverse.1 = bf16[32,4096]{1,0:T(8,128)(2,1)} custom-call(s32[64]{0:T(128)} %flags_ref.3, f32[32,512]{1,0:T(8,128)} %get-tuple-element.46.refs_0_, f32[32,512]{1,0:T(8,128)} %copy-done.11, f32[32,512]{1,0:T(8,128)} %copy-done.10, f32[32,512]{1,0:T(8,128)} %copy-done.9, f32[768,768]{1,0:T(8,128)} %last_panels.1.refs_4_, ...), custom_call_target="tpu_custom_call" | custom-call | tf_op jit(solution)/shard_map/apply_inverse/pallas_call | solution.py:322
  (5 shorter events, 0.1 us)
Async XLA Ops:
  0.0 30.1 %copy-start.8 = (bf16[32,4096]{1,0:T(8,128)(2,1)S(1)}, bf16[32,4096]{1,0:T(8,128)(2,1)}, u32[]{:S(2)}) copy-start(bf16[32,4096]{1,0:T(8,128)(2,1)} %param.4) | copy-start | bytes 786436
  0.0 57.9 %collective-permute-start.10 = (bf16[256,4096]{1,0:T(8,128)(2,1)}, bf16[256,4096]{1,0:T(8,128)(2,1)S(1)}, u32[]{:S(2)}, u32[]{:S(2)}) collective-permute-start(bf16[256,4096]{1,0:T(8,128)(2,1)} %tokens_ref.1), channel_id=1, source_target_pairs={{0,1},{1,0},{2,3},{3,2},{4,5},{5,4},{6,7},{7,6},{8,9},{9,8},{10,11... | collective-permute-start | bytes 6291464 | tf_op jit(solution)/shard_map/ppermute | solution.py:341
  5.5 52.5 %copy-start = (bf16[256,4096]{1,0:T(8,128)(2,1)S(1)}, bf16[256,4096]{1,0:T(8,128)(2,1)}, u32[]{:S(2)}) copy-start(bf16[256,4096]{1,0:T(8,128)(2,1)} %tokens_ref.1) | copy-start | bytes 6291460
  5.5 14.0 %collective-permute-start.5 = (bf16[784,256]{1,0:T(8,128)(2,1)}, bf16[784,256]{1,0:T(8,128)(2,1)S(1)}, u32[]{:S(2)}, u32[]{:S(2)}) collective-permute-start(bf16[784,256]{1,0:T(8,128)(2,1)} %select_kept.1.refs_0_.refs_5_), channel_id=1, source_target_pairs={{0,6},{1,7},{2,4},{3,5},{4,2},{5,3},{6,0},{7,1},{8,14},{9,15},{10,... | collective-permute-start | bytes 1204232 | tf_op jit(solution)/shard_map/ppermute | solution.py:341
  9.1 18.6 %collective-permute-start.3 = (bf16[784,256]{1,0:T(8,128)(2,1)}, bf16[784,256]{1,0:T(8,128)(2,1)S(1)}, u32[]{:S(2)}, u32[]{:S(2)}) collective-permute-start(bf16[784,256]{1,0:T(8,128)(2,1)} %select_kept.1.refs_0_.refs_5_), channel_id=1, source_target_pairs={{0,4},{1,5},{2,6},{3,7},{4,0},{5,1},{6,2},{7,3},{8,12},{9,13},{10,... | collective-permute-start | bytes 1204232 | tf_op jit(solution)/shard_map/ppermute | solution.py:341
  9.6 18.4 %collective-permute-start.1 = (bf16[784,256]{1,0:T(8,128)(2,1)}, bf16[784,256]{1,0:T(8,128)(2,1)S(1)}, u32[]{:S(2)}, u32[]{:S(2)}) collective-permute-start(bf16[784,256]{1,0:T(8,128)(2,1)} %select_kept.1.refs_0_.refs_5_), channel_id=1, source_target_pairs={{0,2},{1,3},{2,0},{3,1},{4,6},{5,7},{6,4},{7,5},{8,10},{9,11},{10,... | collective-permute-start | bytes 1204232 | tf_op jit(solution)/shard_map/ppermute | solution.py:341
  9.8 18.5 %collective-permute-start = (bf16[784,256]{1,0:T(8,128)(2,1)}, bf16[784,256]{1,0:T(8,128)(2,1)S(1)}, u32[]{:S(2)}, u32[]{:S(2)}) collective-permute-start(bf16[784,256]{1,0:T(8,128)(2,1)} %select_kept.1.refs_0_.refs_5_), channel_id=1, source_target_pairs={{0,1},{1,0},{2,3},{3,2},{4,5},{5,4},{6,7},{7,6},{8,9},{9,8},{10,11... | collective-permute-start | bytes 1204232 | tf_op jit(solution)/shard_map/ppermute | solution.py:341
  19.5 14.1 %copy-start.1 = (bf16[784,256]{1,0:T(8,128)(2,1)}, bf16[784,256]{1,0:T(8,128)(2,1)S(1)}, u32[]{:S(2)}) copy-start(bf16[784,256]{1,0:T(8,128)(2,1)S(1)} %collective-permute-done.5.refs_6_.refs_11_) | copy-start | bytes 1204228
  19.5 8.8 %collective-permute-start.6 = (bf16[784,256]{1,0:T(8,128)(2,1)S(1)}, bf16[784,256]{1,0:T(8,128)(2,1)S(1)}, u32[]{:S(2)}, u32[]{:S(2)}) collective-permute-start(bf16[784,256]{1,0:T(8,128)(2,1)S(1)} %collective-permute-done.5.refs_6_.refs_11_), channel_id=1, source_target_pairs={{0,1},{1,0},{2,3},{3,2},{4,5},{5,4},{6,7},{7,6},{8,9},{9,8},{10,11... | collective-permute-start | bytes 1204232 | tf_op jit(solution)/shard_map/ppermute | solution.py:341
  27.8 5.8 %copy-start.2 = (bf16[784,256]{1,0:T(8,128)(2,1)}, bf16[784,256]{1,0:T(8,128)(2,1)S(1)}, u32[]{:S(2)}) copy-start(bf16[784,256]{1,0:T(8,128)(2,1)S(1)} %collective-permute-done.3.refs_4_.refs_9_) | copy-start | bytes 1204228
  27.8 1.7 %collective-permute-start.4 = (bf16[784,256]{1,0:T(8,128)(2,1)S(1)}, bf16[784,256]{1,0:T(8,128)(2,1)S(1)}, u32[]{:S(2)}, u32[]{:S(2)}) collective-permute-start(bf16[784,256]{1,0:T(8,128)(2,1)S(1)} %collective-permute-done.3.refs_4_.refs_9_), channel_id=1, source_target_pairs={{0,1},{1,0},{2,3},{3,2},{4,5},{5,4},{6,7},{7,6},{8,9},{9,8},{10,11... | collective-permute-start | bytes 1204232 | tf_op jit(solution)/shard_map/ppermute | solution.py:341
  28.1 5.5 %copy-start.3 = (bf16[784,256]{1,0:T(8,128)(2,1)}, bf16[784,256]{1,0:T(8,128)(2,1)S(1)}, u32[]{:S(2)}) copy-start(bf16[784,256]{1,0:T(8,128)(2,1)S(1)} %collective-permute-done.1.refs_2_.refs_7_) | copy-start | bytes 1204228
  28.1 2.0 %collective-permute-start.2 = (bf16[784,256]{1,0:T(8,128)(2,1)S(1)}, bf16[784,256]{1,0:T(8,128)(2,1)S(1)}, u32[]{:S(2)}, u32[]{:S(2)}) collective-permute-start(bf16[784,256]{1,0:T(8,128)(2,1)S(1)} %collective-permute-done.1.refs_2_.refs_7_), channel_id=1, source_target_pairs={{0,1},{1,0},{2,3},{3,2},{4,5},{5,4},{6,7},{7,6},{8,9},{9,8},{10,11... | collective-permute-start | bytes 1204232 | tf_op jit(solution)/shard_map/ppermute | solution.py:341
  28.3 5.3 %copy-start.4 = (bf16[784,256]{1,0:T(8,128)(2,1)}, bf16[784,256]{1,0:T(8,128)(2,1)S(1)}, u32[]{:S(2)}) copy-start(bf16[784,256]{1,0:T(8,128)(2,1)S(1)} %collective-permute-done.refs_1_.refs_6_) | copy-start | bytes 1204228
  28.3 5.3 %copy-start.5 = (bf16[784,256]{1,0:T(8,128)(2,1)}, bf16[784,256]{1,0:T(8,128)(2,1)S(1)}, u32[]{:S(2)}) copy-start(bf16[784,256]{1,0:T(8,128)(2,1)S(1)} %collective-permute-done.6.refs_7_.refs_12_) | copy-start | bytes 1204228
  29.5 4.1 %copy-start.6 = (bf16[784,256]{1,0:T(8,128)(2,1)}, bf16[784,256]{1,0:T(8,128)(2,1)S(1)}, u32[]{:S(2)}) copy-start(bf16[784,256]{1,0:T(8,128)(2,1)S(1)} %collective-permute-done.4.refs_5_.refs_10_) | copy-start | bytes 1204228
  30.1 3.5 %copy-start.7 = (bf16[784,256]{1,0:T(8,128)(2,1)}, bf16[784,256]{1,0:T(8,128)(2,1)S(1)}, u32[]{:S(2)}) copy-start(bf16[784,256]{1,0:T(8,128)(2,1)S(1)} %collective-permute-done.2.refs_3_.refs_8_) | copy-start | bytes 1204228
  30.1 27.8 %collective-permute-start.9 = (bf16[32,4096]{1,0:T(8,128)(2,1)S(1)}, bf16[32,4096]{1,0:T(8,128)(2,1)S(1)}, u32[]{:S(2)}, u32[]{:S(2)}) collective-permute-start(bf16[32,4096]{1,0:T(8,128)(2,1)S(1)} %copy-done.8), channel_id=1, source_target_pairs={{0,6},{1,7},{2,4},{3,5},{4,2},{5,3},{6,0},{7,1},{8,14},{9,15},{10,... | collective-permute-start | bytes 786440 | tf_op jit(solution)/shard_map/ppermute | solution.py:341
  31.9 26.0 %collective-permute-start.8 = (bf16[32,4096]{1,0:T(8,128)(2,1)S(1)}, bf16[32,4096]{1,0:T(8,128)(2,1)S(1)}, u32[]{:S(2)}, u32[]{:S(2)}) collective-permute-start(bf16[32,4096]{1,0:T(8,128)(2,1)S(1)} %copy-done.8), channel_id=1, source_target_pairs={{0,4},{1,5},{2,6},{3,7},{4,0},{5,1},{6,2},{7,3},{8,12},{9,13},{10,... | collective-permute-start | bytes 786440 | tf_op jit(solution)/shard_map/ppermute | solution.py:341
  33.2 24.6 %collective-permute-start.7 = (bf16[32,4096]{1,0:T(8,128)(2,1)S(1)}, bf16[32,4096]{1,0:T(8,128)(2,1)S(1)}, u32[]{:S(2)}, u32[]{:S(2)}) collective-permute-start(bf16[32,4096]{1,0:T(8,128)(2,1)S(1)} %copy-done.8), channel_id=1, source_target_pairs={{0,2},{1,3},{2,0},{3,1},{4,6},{5,7},{6,4},{7,5},{8,10},{9,11},{10,... | collective-permute-start | bytes 786440 | tf_op jit(solution)/shard_map/ppermute | solution.py:341
  60.4 24.6 %collective-permute-start.13 = (f32[32,512]{1,0:T(8,128)S(1)}, f32[32,512]{1,0:T(8,128)S(1)}, u32[]{:S(2)}, u32[]{:S(2)}) collective-permute-start(f32[32,512]{1,0:T(8,128)S(1)} %get-tuple-element.43), channel_id=1, source_target_pairs={{0,6},{1,7},{2,4},{3,5},{4,2},{5,3},{6,0},{7,1},{8,14},{9,15},{10,... | collective-permute-start | bytes 196616 | tf_op jit(solution)/shard_map/ppermute | solution.py:341
  62.2 22.8 %collective-permute-start.12 = (f32[32,512]{1,0:T(8,128)S(1)}, f32[32,512]{1,0:T(8,128)S(1)}, u32[]{:S(2)}, u32[]{:S(2)}) collective-permute-start(f32[32,512]{1,0:T(8,128)S(1)} %get-tuple-element.44), channel_id=1, source_target_pairs={{0,4},{1,5},{2,6},{3,7},{4,0},{5,1},{6,2},{7,3},{8,12},{9,13},{10,... | collective-permute-start | bytes 196616 | tf_op jit(solution)/shard_map/ppermute | solution.py:341
  63.5 21.5 %collective-permute-start.11 = (f32[32,512]{1,0:T(8,128)S(1)}, f32[32,512]{1,0:T(8,128)S(1)}, u32[]{:S(2)}, u32[]{:S(2)}) collective-permute-start(f32[32,512]{1,0:T(8,128)S(1)} %get-tuple-element.45), channel_id=1, source_target_pairs={{0,2},{1,3},{2,0},{3,1},{4,6},{5,7},{6,4},{7,5},{8,10},{9,11},{10,... | collective-permute-start | bytes 196616 | tf_op jit(solution)/shard_map/ppermute | solution.py:341
  85.0 0.6 copy-start.9
  85.0 0.6 copy-start.10
  85.0 0.6 copy-start.11

commit v3 on v2

--- a/solution.py
+++ b/solution.py
@@ -58,14 +58,14 @@
         reads[-1].start()
     row = lax.broadcasted_iota(jnp.int32, (width, 128), 0)
     lane = lax.broadcasted_iota(jnp.int32, (width, 128), 1)
+    for copy in tiles + reads:
+        copy.wait()
     for i in range(KEEP_BLK):
         inner = (index_ref[i] % per_tile) * width
         pick = jnp.where(lane == row + inner, 1.0, 0.0).astype(jnp.bfloat16)
-        tiles[i].wait()
         out_ref[i * width:(i + 1) * width, :] = dot32(pick, tile_ref[i], NT).astype(jnp.bfloat16)
     total = jnp.zeros((step, 128), jnp.float32)
     for c in range(chunks):
-        reads[c].wait()
         for f in range(features // 128):
             piece = chunk_ref[c, :, f * 128:(f + 1) * 128].astype(jnp.float32)
             total += piece * piece
@@ -120,23 +120,28 @@
     return terms[0]
 
 
-def invert_small(cols, sub):
-    cols = list(cols)
-    r = pl.reciprocal(sublane_row(cols[0], 0), approx=True)
+def sweep_small(block):
+    entry = {}
+    for j in range(SUB):
+        column = lane_column(block[0], block[1] + j)
+        for i in range(j + 1):
+            entry[i, j] = sublane_row(column, i)
+    r = pl.reciprocal(entry[0, 0], approx=True)
     for t in range(SUB):
-        here = sub == t
         after = None
         if t + 1 < SUB:
-            product = sublane_row(cols[t + 1], t) * sublane_row(cols[t], t + 1)
-            after = pl.reciprocal(sublane_row(cols[t + 1], t + 1) - product * r, approx=True)
-        pivot_col = jnp.where(here, -1.0, cols[t])
+            square = entry[t, t + 1] * entry[t, t + 1]
+            after = pl.reciprocal(entry[t + 1, t + 1] - square * r, approx=True)
+        line = [entry[min(i, t), max(i, t)] for i in range(SUB)]
+        scaled = [line[i] * r for i in range(SUB)]
         for j in range(SUB):
-            if j != t:
-                w = sublane_row(cols[j], t) * r
-                cols[j] = jnp.where(here, 0.0, cols[j]) - pivot_col * w
-        cols[t] = -(pivot_col * r)
+            for i in range(j + 1):
+                if i != t and j != t:
+                    entry[i, j] = entry[i, j] - line[i] * scaled[j]
+        for i in range(SUB):
+            entry[min(i, t), max(i, t)] = -r if i == t else scaled[i]
         r = after
-    return cols
+    return entry
 
 
 def invert_panel(block):
@@ -148,14 +153,19 @@
     for s in range(count):
         base = s * SUB
         inside = (lane >= base) & (lane < base + SUB)
-        cols = invert_small([lane_column(rows[s], base + j) for j in range(SUB)], sub)
+        entry = sweep_small((rows[s], base))
         pivot_rows = jnp.where(inside, jnp.where(lane == sub + base, 1.0, 0.0), rows[s])
-        new = tree_sum([cols[j] * sublane_row(pivot_rows, j) for j in range(SUB)])
-        spread = [sublane_row(new, j) for j in range(SUB)]
+        spread_in = [sublane_row(pivot_rows, j) for j in range(SUB)]
+        spread = [
+            tree_sum([entry[min(i, j), max(i, j)] * spread_in[j] for j in range(SUB)]) for i in range(SUB)
+        ]
         for i in [(s + d) % count for d in range(1, count)]:
             change = tree_sum([lane_column(rows[i], base + j) * spread[j] for j in range(SUB)])
-            rows[i] = jnp.where(inside, 0.0, rows[i]) - change
-        rows[s] = new
+            rows[i] = jnp.where(inside, 0.0, rows[i]) + change
+        new = spread[SUB - 1]
+        for j in range(SUB - 1):
+            new = jnp.where(sub == j, spread[j], new)
+        rows[s] = -new
     return jnp.concatenate(rows, axis=0)
 
 
@@ -196,25 +206,31 @@
         a_ref[:, c:c + 256] = value if scale is None else value * scale
 
 
-def first_kernel(features, last, *refs):
+def place_pieces(pieces, all_ref, sem):
+    copies = []
+    at = 0
+    for k, piece in enumerate(pieces):
+        width = piece.shape[1]
+        copies.append(pltpu.make_async_copy(piece, all_ref.at[:, at:at + width], sem.at[k]))
+        copies[-1].start()
+        at += width
+    return copies
+
+
+def first_kernel(features, rows, last, *refs):
     pieces = refs[:-6]
     out_ref, scale_ref, all_ref, left_ref, right_ref, sem = refs[-6:]
-    n = len(pieces)
     kept = out_ref.shape[0]
-    rows = pieces[0].shape[1]
-    copies = [
-        pltpu.make_async_copy(pieces[k], all_ref.at[:, k * rows:(k + 1) * rows], sem.at[k]) for k in range(n)
-    ]
-    for copy in copies:
-        copy.start()
+    copies = place_pieces(pieces, all_ref, sem)
     for copy in copies:
         copy.wait()
+    tokens = all_ref.shape[1]
     total = jnp.float32(0.0)
-    for k in range(n):
-        total = total + jnp.sum(all_ref[kept:, k * rows:k * rows + 1].astype(jnp.float32))
+    for k in range(0, tokens, rows):
+        total = total + jnp.sum(all_ref[kept:, k:k + 1].astype(jnp.float32))
     scale_ref[...] = 1.0 / jnp.full(scale_ref.shape, 0.01 * total / features, jnp.float32)
     scale = scale_ref[0:1, 0:1]
-    chunk = 2048 if (n * rows) % 2048 == 0 else rows
+    chunk = 2048 if tokens % 2048 == 0 else rows
     tile = 256
     unit = lax.broadcasted_iota(jnp.int32, (kept, tile), 0) - lax.broadcasted_iota(jnp.int32, (kept, tile), 1)
 
@@ -222,7 +238,7 @@
     def _(j):
         at = pl.multiple_of(j * tile, tile)
         acc = jnp.where(unit == at, 1.0, 0.0)
-        for c in range(0, n * rows, chunk):
+        for c in range(0, tokens, chunk):
             part = dot32(all_ref[:kept, c:c + chunk], all_ref[pl.ds(at, tile), c:c + chunk], NT)
             acc = acc + part * scale
         out_ref[:, pl.ds(at, tile)] = acc
@@ -234,8 +250,9 @@
     kept_extra, rows = pieces[0].shape
     kept = kept_extra - EXTRA
     n = len(pieces)
+    tokens = sum(piece.shape[1] for piece in pieces)
     return pl.pallas_call(
-        functools.partial(first_kernel, float(features), last),
+        functools.partial(first_kernel, float(features), rows, last),
         out_shape=[
             jax.ShapeDtypeStruct((kept, kept), jnp.float32),
             jax.ShapeDtypeStruct((8, 128), jnp.float32),
@@ -243,7 +260,7 @@
         in_specs=[pl.BlockSpec(memory_space=pl.ANY)] * n,
         out_specs=[pl.BlockSpec(memory_space=pltpu.VMEM)] * 2,
         scratch_shapes=[
-            pltpu.VMEM((kept_extra, n * rows), jnp.bfloat16),
+            pltpu.VMEM((kept_extra, tokens), jnp.bfloat16),
             pltpu.VMEM((kept, 6 * PANEL), jnp.bfloat16),
             pltpu.VMEM((6 * PANEL, kept), jnp.bfloat16),
             pltpu.SemaphoreType.DMA((n,)),
@@ -279,27 +296,30 @@
 def apply_kernel(chips, flags_ref, *refs):
     projected, refs = refs[:chips], refs[chips:]
     inverse_ref, refs = refs[0], refs[1:]
-    pieces, (out_ref, index_ref, wide_ref) = refs[:2 * chips], refs[2 * chips:]
+    pieces, (out_ref, index_ref, wide_ref, all_ref, held_ref, sem, held_sem) = refs[:-7], refs[-7:]
     own, features = out_ref.shape
     blocks = flags_ref.shape[0]
     width = features // blocks
     per_tile = 128 // width
     kept = inverse_ref.shape[0]
-    rows = pieces[0].shape[1]
+    fetch = pltpu.make_async_copy(inverse_ref, held_ref, held_sem)
+    fetch.start()
+    copies = place_pieces(pieces, all_ref, sem)
     kept_blocks(flags_ref, index_ref)
-    right = jnp.zeros((3 * own, kept), jnp.float32)
-    for k in range(chips):
-        for core in range(2):
-            hi, mid, low = split3(projected[k][:, core * rows:(core + 1) * rows])
-            right += dot32(jnp.concatenate([hi, mid, low], axis=0), pieces[2 * k + core][:kept, :], NT)
+    wide_ref[...] = jnp.zeros((own, features), jnp.float32)
+    split = [split3(part[...]) for part in projected]
+    left = jnp.concatenate([jnp.concatenate([s[i] for s in split], axis=1) for i in range(3)], axis=0)
+    fetch.wait()
+    for copy in copies:
+        copy.wait()
+    right = dot32(left, all_ref[:kept, :], NT)
     right = right[:own] + right[own:2 * own] + right[2 * own:]
     hi, mid, low = split3(right)
-    ihi, imid, ilow = split3(inverse_ref[...])
+    ihi, imid, ilow = split3(held_ref[...])
     first = dot32(jnp.concatenate([hi, mid, low], axis=0), ihi, NN)
     second = dot32(jnp.concatenate([hi, mid], axis=0), imid, NN)
     third = dot32(hi, ilow, NN)
     answer = first[:own] + first[own:2 * own] + second[:own] + first[2 * own:] + second[own:] + third
-    wide_ref[...] = jnp.zeros((own, features), jnp.float32)
     place = lax.broadcasted_iota(jnp.int32, (own, 128), 1) // width
     for i in range(KEEP_BLK):
         b = index_ref[i]
@@ -318,15 +338,22 @@
     own = projected[0].shape[0]
     blocks = keep_flags.shape[0]
     chips = len(projected)
+    kept = inverse.shape[0]
+    tokens = sum(piece.shape[1] for piece in pieces)
     vmem = pl.BlockSpec(memory_space=pltpu.VMEM)
+    anywhere = pl.BlockSpec(memory_space=pl.ANY)
     return pl.pallas_call(
         functools.partial(apply_kernel, chips),
         out_shape=jax.ShapeDtypeStruct((own, features), jnp.bfloat16),
-        in_specs=[pl.BlockSpec(memory_space=pltpu.SMEM)] + [vmem] * (1 + 3 * chips),
+        in_specs=[pl.BlockSpec(memory_space=pltpu.SMEM)] + [vmem] * chips + [anywhere] * (1 + len(pieces)),
         out_specs=vmem,
         scratch_shapes=[
             pltpu.SMEM((blocks + 1,), jnp.int32),
             pltpu.VMEM((own, features), jnp.float32),
+            pltpu.VMEM((kept + EXTRA, tokens), jnp.bfloat16),
+            pltpu.VMEM((kept, kept), jnp.float32),
+            pltpu.SemaphoreType.DMA((len(pieces),)),
+            pltpu.SemaphoreType.DMA,
         ],
         compiler_params=pltpu.CompilerParams(vmem_limit_bytes=VMEM_LIMIT),
         name="apply_inverse",
@@ -339,6 +366,14 @@
 
     def swap(x, k):
         return lax.ppermute(x, "dp", [(d, d ^ k) for d in range(n)])
+
+    def gather_kept(kept):
+        if n != 8:
+            return [[kept]] + [[swap(kept, k)] for k in others]
+        near = [swap(kept, 2), swap(kept, 4)]
+        middle = kept.shape[1] // 2
+        far = [swap(near[0][:, :middle], 4), swap(near[1][:, middle:], 2)]
+        return [[kept], [near[0]], [near[1]], far]
 
     def on_device(tokens, orig_weight, keep_flags):
         features = tokens.shape[1]
@@ -346,11 +381,11 @@
         kept = select_kept(tokens, keep_flags)
         panels = (kept.shape[0] - EXTRA) // PANEL
         half = panels // 2
-        same = [kept] + [swap(kept, k) for k in others]
+        same = gather_kept(kept)
+        same[-1], orig_weight = lax.optimization_barrier((same[-1], orig_weight))
         pieces = []
-        for piece in same:
-            pieces += [piece, swap(piece, 1)]
-        pieces, orig_weight = lax.optimization_barrier((pieces, orig_weight))
+        for group in same:
+            pieces += group + [swap(piece, 1) for piece in group]
         sibling = swap(tokens, 1)
         weights = [orig_weight] + [swap(orig_weight, k) for k in others]
         begun, scale = first_half(pieces, features, half)

time: 91.8 us -> 92.4 us (level)
  waiting for transfers between devices: 20 us -> 13.2 us
  starting transfers between devices: 12 us -> 15.7 us
  Pallas kernels: 56.3 us -> 59 us
    ppermute x14 -> x16, waiting for transfers between devices: 20 us -> 13.2 us  [swap(): return lax.ppermute(x, 'dp', [(d, d ^ k) for d in range(n)])]
    ppermute x14 -> x16, starting transfers between devices: 12 us -> 15.7 us  [swap(): return lax.ppermute(x, 'dp', [(d, d ^ k) for d in range(n)])]
    pallas_call x1, Pallas kernels: 24.2 us -> 25.5 us  [first_half(): pl.pallas_call(functools.partial(first_kernel, float(features), rows, las...]
    pallas_call x1, Pallas kernels: 21.1 us -> 22.3 us  [second_half(): pl.pallas_call(functools.partial(second_kernel, first), out_shape=jax.Sha...]
    pallas_call x1, Pallas kernels: 5.96 us -> 6.93 us  [apply_inverse(): pl.pallas_call(functools.partial(apply_kernel, chips), out_shape=jax.Shap...]
  transfers between devices with their start and end apart: 14 -> 16, of which waited for: 5 -> 3; matrix products, arithmetic and copies ran while one was open for 0% -> 0% of each run, Pallas kernels for 55% -> 57%
where the time goes in v3:
time: 92.4 us; the launch traced here: 92.1 us
  Pallas kernels  59 us (64%)
  starting transfers between devices  15.7 us (17%)
  waiting for transfers between devices  13.2 us (14%)
  local copies, waits for them, and re-layouts  2.18 us (2%)
  matrix products  1.67 us (2%)
    pallas_call x1, Pallas kernels, first_half(): pl.pallas_call(functools.partial(first_kernel, float(features), rows, las...  25.5 us
    pallas_call x1, Pallas kernels, second_half(): pl.pallas_call(functools.partial(second_kernel, first), out_shape=jax.Sha...  22.3 us
    ppermute x16, starting transfers between devices, swap(): return lax.ppermute(x, 'dp', [(d, d ^ k) for d in range(n)])  15.7 us
    ppermute x16, waiting for transfers between devices, swap(): return lax.ppermute(x, 'dp', [(d, d ^ k) for d in range(n)])  13.2 us
    pallas_call x1, Pallas kernels, apply_inverse(): pl.pallas_call(functools.partial(apply_kernel, chips), out_shape=jax.Shap...  6.93 us
    pallas_call x1, Pallas kernels, select_kept(): pl.pallas_call(select_kernel, out_shape=jax.ShapeDtypeStruct((kept + EXTR...  4.25 us
  transfers between devices with their start and end apart: 16, of which 3 were waited for; matrix products, arithmetic and copies ran while one was open for 0% of the time, Pallas kernels for 57%

profile of v3, /device:TPU:0, one launch (start us, length us, event | category | flops | bytes accessed | tf_op | source)
XLA Modules:
  0.0 92.1 jit_solution(16769134795287885225)
XLA Ops:
  0.0 0.0 copy-start.10
  0.0 0.5 collective-permute-start.12
  0.5 4.3 %select_kept.1.refs_0_.refs_5_ = bf16[784,256]{1,0:T(8,128)(2,1)} custom-call(s32[64]{0:T(128)} %flags_ref.3, bf16[256,4096]{1,0:T(8,128)(2,1)} %tokens_ref.1), custom_call_target="tpu_custom_call" | custom-call | tf_op jit(solution)/shard_map/select_kept/pallas_call | solution.py:88
  4.7 2.7 %collective-permute-start.3 = (bf16[784,256]{1,0:T(8,128)(2,1)}, bf16[784,256]{1,0:T(8,128)(2,1)S(1)}, u32[]{:S(2)}, u32[]{:S(2)}) collective-permute-start(bf16[784,256]{1,0:T(8,128)(2,1)} %select_kept.1.refs_0_.refs_5_), channel_id=1, source_target_pairs={{0,4},{1,5},{2,6},{3,7},{4,0},{5,1},{6,2},{7,3},{8,12},{9,13},{10,... | collective-permute-start | bytes 1204232 | tf_op jit(solution)/shard_map/ppermute | solution.py:368
  7.4 1.5 %collective-permute-start.1 = (bf16[784,256]{1,0:T(8,128)(2,1)}, bf16[784,256]{1,0:T(8,128)(2,1)S(1)}, u32[]{:S(2)}, u32[]{:S(2)}) collective-permute-start(bf16[784,256]{1,0:T(8,128)(2,1)} %select_kept.1.refs_0_.refs_5_), channel_id=1, source_target_pairs={{0,2},{1,3},{2,0},{3,1},{4,6},{5,7},{6,4},{7,5},{8,10},{9,11},{10,... | collective-permute-start | bytes 1204232 | tf_op jit(solution)/shard_map/ppermute | solution.py:368
  8.9 0.0 collective-permute-start
  8.9 8.5 %collective-permute-done.3.refs_4_.refs_9_ = bf16[784,256]{1,0:T(8,128)(2,1)S(1)} collective-permute-done((bf16[784,256]{1,0:T(8,128)(2,1)}, bf16[784,256]{1,0:T(8,128)(2,1)S(1)}, u32[]{:S(2)}, u32[]{:S(2)}) %collective-permute-start.3) | collective-permute-done | bytes 401440 | tf_op jit(solution)/shard_map/ppermute | solution.py:368
  17.5 0.0 copy-start.1
  17.5 1.8 %collective-permute-start.6 = (bf16[784,128]{1,0:T(8,128)(2,1)S(1)}, bf16[784,128]{1,0:T(8,128)(2,1)S(1)}, u32[]{:S(2)}, u32[]{:S(2)}) collective-permute-start(bf16[784,128]{1,0:T(8,128)(2,1)S(1)} %slice.25), channel_id=1, source_target_pairs={{0,2},{1,3},{2,0},{3,1},{4,6},{5,7},{6,4},{7,5},{8,10},{9,11},{10,... | collective-permute-start | bytes 602120 | tf_op jit(solution)/shard_map/ppermute | solution.py:368
  19.3 0.0 collective-permute-done.1.refs_2_.refs_7_
  19.3 0.0 copy-start.2
  19.3 0.0 copy-start
  19.3 1.6 %collective-permute-start.5 = (bf16[784,128]{1,0:T(8,128)(2,1)S(1)}, bf16[784,128]{1,0:T(8,128)(2,1)S(1)}, u32[]{:S(2)}, u32[]{:S(2)}) collective-permute-start(bf16[784,128]{1,0:T(8,128)(2,1)S(1)} %slice.24), channel_id=1, source_target_pairs={{0,4},{1,5},{2,6},{3,7},{4,0},{5,1},{6,2},{7,3},{8,12},{9,13},{10,... | collective-permute-start | bytes 602120 | tf_op jit(solution)/shard_map/ppermute | solution.py:368
  20.9 0.0 collective-permute-start.4
  20.9 3.4 %collective-permute-done.6.refs_7_.refs_12_ = bf16[784,128]{1,0:T(8,128)(2,1)S(1)} collective-permute-done((bf16[784,128]{1,0:T(8,128)(2,1)S(1)}, bf16[784,128]{1,0:T(8,128)(2,1)S(1)}, u32[]{:S(2)}, u32[]{:S(2)}) %collective-permute-start.6) | collective-permute-done | bytes 200736 | tf_op jit(solution)/shard_map/ppermute | solution.py:368
  24.3 0.0 copy-start.6
  24.3 1.3 %collective-permute-done.5.refs_6_.refs_11_ = bf16[784,128]{1,0:T(8,128)(2,1)S(1)} collective-permute-done((bf16[784,128]{1,0:T(8,128)(2,1)S(1)}, bf16[784,128]{1,0:T(8,128)(2,1)S(1)}, u32[]{:S(2)}, u32[]{:S(2)}) %collective-permute-start.5) | collective-permute-done | bytes 200736 | tf_op jit(solution)/shard_map/ppermute | solution.py:368
  25.5 0.0 copy-start.7
  25.6 0.0 collective-permute-start.7
  25.6 0.5 collective-permute-start.8
  26.1 0.0 collective-permute-done.refs_1_.refs_6_
  26.1 0.0 copy-start.3
  26.1 0.1 collective-permute-start.2
  26.1 0.0 collective-permute-done.4.refs_5_.refs_10_
  26.1 0.0 copy-done.10
  26.1 0.0 copy-start.4
  26.1 1.6 %collective-permute-start.11 = (bf16[32,4096]{1,0:T(8,128)(2,1)S(1)}, bf16[32,4096]{1,0:T(8,128)(2,1)S(1)}, u32[]{:S(2)}, u32[]{:S(2)}) collective-permute-start(bf16[32,4096]{1,0:T(8,128)(2,1)S(1)} %copy-done.10), channel_id=1, source_target_pairs={{0,6},{1,7},{2,4},{3,5},{4,2},{5,3},{6,0},{7,1},{8,14},{9,15},{10,... | collective-permute-start | bytes 786440 | tf_op jit(solution)/shard_map/ppermute | solution.py:368
  27.7 0.0 collective-permute-done.7.refs_8_.refs_13_
  27.7 1.1 %collective-permute-start.10 = (bf16[32,4096]{1,0:T(8,128)(2,1)S(1)}, bf16[32,4096]{1,0:T(8,128)(2,1)S(1)}, u32[]{:S(2)}, u32[]{:S(2)}) collective-permute-start(bf16[32,4096]{1,0:T(8,128)(2,1)S(1)} %copy-done.10), channel_id=1, source_target_pairs={{0,4},{1,5},{2,6},{3,7},{4,0},{5,1},{6,2},{7,3},{8,12},{9,13},{10,... | collective-permute-start | bytes 786440 | tf_op jit(solution)/shard_map/ppermute | solution.py:368
  28.8 0.0 collective-permute-done.8.refs_9_.refs_14_
  28.8 0.9 %collective-permute-start.9 = (bf16[32,4096]{1,0:T(8,128)(2,1)S(1)}, bf16[32,4096]{1,0:T(8,128)(2,1)S(1)}, u32[]{:S(2)}, u32[]{:S(2)}) collective-permute-start(bf16[32,4096]{1,0:T(8,128)(2,1)S(1)} %copy-done.10), channel_id=1, source_target_pairs={{0,2},{1,3},{2,0},{3,1},{4,6},{5,7},{6,4},{7,5},{8,10},{9,11},{10,... | collective-permute-start | bytes 786440 | tf_op jit(solution)/shard_map/ppermute | solution.py:368
  29.7 0.0 collective-permute-done.2.refs_3_.refs_8_
  29.7 0.0 copy-done.1
  29.7 0.0 copy-done.2
  29.7 0.0 copy-done.6
  29.7 0.0 copy-done.7
  29.7 0.0 copy-done.3
  29.7 0.0 copy-done.4
  29.8 0.0 copy-done.8
  29.8 0.0 copy-done.9
  29.8 0.0 copy-start.5
  29.8 0.8 copy-done.5
  30.5 25.5 %gram_and_first_panels.1 = (f32[768,768]{1,0:T(8,128)}, f32[8,128]{1,0:T(8,128)}) custom-call(bf16[784,256]{1,0:T(8,128)(2,1)} %select_kept.1.refs_0_.refs_5_, bf16[784,256]{1,0:T(8,128)(2,1)} %copy-done.3, bf16[784,256]{1,0:T(8,128)(2,1)} %copy-done.2, bf16[784,256]{1,0:T(8,128)(2,1)} %copy-done.5, bf16[784,256]{1,0:T(8,128)(2,1)} %copy-done.1, ...), custom_call_target="tpu_custom_call" | custom-call | tf_op jit(solution)/shard_map/gram_and_first_panels/pallas_call | solution.py:254
  56.0 0.0 collective-permute-done.11
  56.0 0.0 collective-permute-done.10
  56.0 0.0 collective-permute-done.9
  56.0 0.0 collective-permute-done.12
  56.2 0.0 copy-done
  56.2 0.8 fusion.1
  57.0 0.8 fusion.2
  57.9 0.6 fusion
  58.5 1.6 %collective-permute-start.15 = (f32[32,512]{1,0:T(8,128)S(1)}, f32[32,512]{1,0:T(8,128)S(1)}, u32[]{:S(2)}, u32[]{:S(2)}) collective-permute-start(f32[32,512]{1,0:T(8,128)S(1)} %get-tuple-element.31), channel_id=1, source_target_pairs={{0,6},{1,7},{2,4},{3,5},{4,2},{5,3},{6,0},{7,1},{8,14},{9,15},{10,... | collective-permute-start | bytes 196616 | tf_op jit(solution)/shard_map/ppermute | solution.py:368
  60.1 1.0 %collective-permute-start.14 = (f32[32,512]{1,0:T(8,128)S(1)}, f32[32,512]{1,0:T(8,128)S(1)}, u32[]{:S(2)}, u32[]{:S(2)}) collective-permute-start(f32[32,512]{1,0:T(8,128)S(1)} %get-tuple-element.32), channel_id=1, source_target_pairs={{0,4},{1,5},{2,6},{3,7},{4,0},{5,1},{6,2},{7,3},{8,12},{9,13},{10,... | collective-permute-start | bytes 196616 | tf_op jit(solution)/shard_map/ppermute | solution.py:368
  61.1 0.9 %collective-permute-start.13 = (f32[32,512]{1,0:T(8,128)S(1)}, f32[32,512]{1,0:T(8,128)S(1)}, u32[]{:S(2)}, u32[]{:S(2)}) collective-permute-start(f32[32,512]{1,0:T(8,128)S(1)} %get-tuple-element.33), channel_id=1, source_target_pairs={{0,2},{1,3},{2,0},{3,1},{4,6},{5,7},{6,4},{7,5},{8,10},{9,11},{10,... | collective-permute-start | bytes 196616 | tf_op jit(solution)/shard_map/ppermute | solution.py:368
  62.0 22.3 %last_panels.1.refs_4_ = f32[768,768]{1,0:T(8,128)} custom-call(f32[768,768]{1,0:T(8,128)} %get-tuple-element.29.a_ref, f32[8,128]{1,0:T(8,128)} %get-tuple-element.30.scale_ref), custom_call_target="tpu_custom_call" | custom-call | tf_op jit(solution)/shard_map/last_panels/pallas_call | solution.py:282
  84.3 0.0 collective-permute-done.15.refs_3_
  84.3 0.0 collective-permute-done.14.refs_2_
  84.3 0.0 copy-start.12
  84.4 0.0 collective-permute-done.13.refs_1_
  84.4 0.0 copy-start.13
  84.4 0.6 copy-done.11
  85.0 0.0 copy-done.12
  85.0 0.0 copy-done.13
  85.0 6.9 %apply_inverse.1 = bf16[32,4096]{1,0:T(8,128)(2,1)} custom-call(s32[64]{0:T(128)} %flags_ref.3, f32[32,512]{1,0:T(8,128)} %get-tuple-element.34.refs_0_, f32[32,512]{1,0:T(8,128)} %copy-done.13, f32[32,512]{1,0:T(8,128)} %copy-done.12, f32[32,512]{1,0:T(8,128)} %copy-done.11, f32[768,768]{1,0:T(8,128)} %last_panels.1.refs_4_, ...), custom_call_target="tpu_custom_call" | custom-call | tf_op jit(solution)/shard_map/apply_inverse/pallas_call | solution.py:345
  (10 shorter events, 0.1 us)
Async XLA Ops:
  0.0 26.1 %copy-start.10 = (bf16[32,4096]{1,0:T(8,128)(2,1)S(1)}, bf16[32,4096]{1,0:T(8,128)(2,1)}, u32[]{:S(2)}) copy-start(bf16[32,4096]{1,0:T(8,128)(2,1)} %param.4) | copy-start | bytes 786436
  0.0 56.0 %collective-permute-start.12 = (bf16[256,4096]{1,0:T(8,128)(2,1)}, bf16[256,4096]{1,0:T(8,128)(2,1)S(1)}, u32[]{:S(2)}, u32[]{:S(2)}) collective-permute-start(bf16[256,4096]{1,0:T(8,128)(2,1)} %tokens_ref.1), channel_id=1, source_target_pairs={{0,1},{1,0},{2,3},{3,2},{4,5},{5,4},{6,7},{7,6},{8,9},{9,8},{10,11... | collective-permute-start | bytes 6291464 | tf_op jit(solution)/shard_map/ppermute | solution.py:368
  4.7 12.8 %collective-permute-start.3 = (bf16[784,256]{1,0:T(8,128)(2,1)}, bf16[784,256]{1,0:T(8,128)(2,1)S(1)}, u32[]{:S(2)}, u32[]{:S(2)}) collective-permute-start(bf16[784,256]{1,0:T(8,128)(2,1)} %select_kept.1.refs_0_.refs_5_), channel_id=1, source_target_pairs={{0,4},{1,5},{2,6},{3,7},{4,0},{5,1},{6,2},{7,3},{8,12},{9,13},{10,... | collective-permute-start | bytes 1204232 | tf_op jit(solution)/shard_map/ppermute | solution.py:368
  7.4 11.8 %collective-permute-start.1 = (bf16[784,256]{1,0:T(8,128)(2,1)}, bf16[784,256]{1,0:T(8,128)(2,1)S(1)}, u32[]{:S(2)}, u32[]{:S(2)}) collective-permute-start(bf16[784,256]{1,0:T(8,128)(2,1)} %select_kept.1.refs_0_.refs_5_), channel_id=1, source_target_pairs={{0,2},{1,3},{2,0},{3,1},{4,6},{5,7},{6,4},{7,5},{8,10},{9,11},{10,... | collective-permute-start | bytes 1204232 | tf_op jit(solution)/shard_map/ppermute | solution.py:368
  8.9 17.1 %collective-permute-start = (bf16[784,256]{1,0:T(8,128)(2,1)}, bf16[784,256]{1,0:T(8,128)(2,1)S(1)}, u32[]{:S(2)}, u32[]{:S(2)}) collective-permute-start(bf16[784,256]{1,0:T(8,128)(2,1)} %select_kept.1.refs_0_.refs_5_), channel_id=1, source_target_pairs={{0,1},{1,0},{2,3},{3,2},{4,5},{5,4},{6,7},{7,6},{8,9},{9,8},{10,11... | collective-permute-start | bytes 1204232 | tf_op jit(solution)/shard_map/ppermute | solution.py:368
  17.5 12.2 %copy-start.1 = (bf16[784,256]{1,0:T(8,128)(2,1)}, bf16[784,256]{1,0:T(8,128)(2,1)S(1)}, u32[]{:S(2)}) copy-start(bf16[784,256]{1,0:T(8,128)(2,1)S(1)} %collective-permute-done.3.refs_4_.refs_9_) | copy-start | bytes 1204228
  17.5 6.8 %collective-permute-start.6 = (bf16[784,128]{1,0:T(8,128)(2,1)S(1)}, bf16[784,128]{1,0:T(8,128)(2,1)S(1)}, u32[]{:S(2)}, u32[]{:S(2)}) collective-permute-start(bf16[784,128]{1,0:T(8,128)(2,1)S(1)} %slice.25), channel_id=1, source_target_pairs={{0,2},{1,3},{2,0},{3,1},{4,6},{5,7},{6,4},{7,5},{8,10},{9,11},{10,... | collective-permute-start | bytes 602120 | tf_op jit(solution)/shard_map/ppermute | solution.py:368
  19.3 10.4 %copy-start.2 = (bf16[784,256]{1,0:T(8,128)(2,1)}, bf16[784,256]{1,0:T(8,128)(2,1)S(1)}, u32[]{:S(2)}) copy-start(bf16[784,256]{1,0:T(8,128)(2,1)S(1)} %collective-permute-done.1.refs_2_.refs_7_) | copy-start | bytes 1204228
  19.3 36.9 %copy-start = (bf16[256,4096]{1,0:T(8,128)(2,1)S(1)}, bf16[256,4096]{1,0:T(8,128)(2,1)}, u32[]{:S(2)}) copy-start(bf16[256,4096]{1,0:T(8,128)(2,1)} %tokens_ref.1) | copy-start | bytes 6291460
  19.3 6.2 %collective-permute-start.5 = (bf16[784,128]{1,0:T(8,128)(2,1)S(1)}, bf16[784,128]{1,0:T(8,128)(2,1)S(1)}, u32[]{:S(2)}, u32[]{:S(2)}) collective-permute-start(bf16[784,128]{1,0:T(8,128)(2,1)S(1)} %slice.24), channel_id=1, source_target_pairs={{0,4},{1,5},{2,6},{3,7},{4,0},{5,1},{6,2},{7,3},{8,12},{9,13},{10,... | collective-permute-start | bytes 602120 | tf_op jit(solution)/shard_map/ppermute | solution.py:368
  20.9 5.3 %collective-permute-start.4 = (bf16[784,256]{1,0:T(8,128)(2,1)S(1)}, bf16[784,256]{1,0:T(8,128)(2,1)S(1)}, u32[]{:S(2)}, u32[]{:S(2)}) collective-permute-start(bf16[784,256]{1,0:T(8,128)(2,1)S(1)} %collective-permute-done.3.refs_4_.refs_9_), channel_id=1, source_target_pairs={{0,1},{1,0},{2,3},{3,2},{4,5},{5,4},{6,7},{7,6},{8,9},{9,8},{10,11... | collective-permute-start | bytes 1204232 | tf_op jit(solution)/shard_map/ppermute | solution.py:368
  24.3 5.5 %copy-start.6 = (bf16[784,128]{1,0:T(8,128)(2,1)}, bf16[784,128]{1,0:T(8,128)(2,1)S(1)}, u32[]{:S(2)}) copy-start(bf16[784,128]{1,0:T(8,128)(2,1)S(1)} %collective-permute-done.6.refs_7_.refs_12_) | copy-start | bytes 602116
  25.5 4.2 %copy-start.7 = (bf16[784,128]{1,0:T(8,128)(2,1)}, bf16[784,128]{1,0:T(8,128)(2,1)S(1)}, u32[]{:S(2)}) copy-start(bf16[784,128]{1,0:T(8,128)(2,1)S(1)} %collective-permute-done.5.refs_6_.refs_11_) | copy-start | bytes 602116
  25.6 2.2 %collective-permute-start.7 = (bf16[784,128]{1,0:T(8,128)(2,1)S(1)}, bf16[784,128]{1,0:T(8,128)(2,1)S(1)}, u32[]{:S(2)}, u32[]{:S(2)}) collective-permute-start(bf16[784,128]{1,0:T(8,128)(2,1)S(1)} %collective-permute-done.5.refs_6_.refs_11_), channel_id=1, source_target_pairs={{0,1},{1,0},{2,3},{3,2},{4,5},{5,4},{6,7},{7,6},{8,9},{9,8},{10,11... | collective-permute-start | bytes 602120 | tf_op jit(solution)/shard_map/ppermute | solution.py:368
  25.6 3.2 %collective-permute-start.8 = (bf16[784,128]{1,0:T(8,128)(2,1)S(1)}, bf16[784,128]{1,0:T(8,128)(2,1)S(1)}, u32[]{:S(2)}, u32[]{:S(2)}) collective-permute-start(bf16[784,128]{1,0:T(8,128)(2,1)S(1)} %collective-permute-done.6.refs_7_.refs_12_), channel_id=1, source_target_pairs={{0,1},{1,0},{2,3},{3,2},{4,5},{5,4},{6,7},{7,6},{8,9},{9,8},{10,11... | collective-permute-start | bytes 602120 | tf_op jit(solution)/shard_map/ppermute | solution.py:368
  26.1 3.7 %copy-start.3 = (bf16[784,256]{1,0:T(8,128)(2,1)}, bf16[784,256]{1,0:T(8,128)(2,1)S(1)}, u32[]{:S(2)}) copy-start(bf16[784,256]{1,0:T(8,128)(2,1)S(1)} %collective-permute-done.refs_1_.refs_6_) | copy-start | bytes 1204228
  26.1 3.6 %collective-permute-start.2 = (bf16[784,256]{1,0:T(8,128)(2,1)S(1)}, bf16[784,256]{1,0:T(8,128)(2,1)S(1)}, u32[]{:S(2)}, u32[]{:S(2)}) collective-permute-start(bf16[784,256]{1,0:T(8,128)(2,1)S(1)} %collective-permute-done.1.refs_2_.refs_7_), channel_id=1, source_target_pairs={{0,1},{1,0},{2,3},{3,2},{4,5},{5,4},{6,7},{7,6},{8,9},{9,8},{10,11... | collective-permute-start | bytes 1204232 | tf_op jit(solution)/shard_map/ppermute | solution.py:368
  26.1 3.6 %copy-start.4 = (bf16[784,256]{1,0:T(8,128)(2,1)}, bf16[784,256]{1,0:T(8,128)(2,1)S(1)}, u32[]{:S(2)}) copy-start(bf16[784,256]{1,0:T(8,128)(2,1)S(1)} %collective-permute-done.4.refs_5_.refs_10_) | copy-start | bytes 1204228
  26.1 29.9 %collective-permute-start.11 = (bf16[32,4096]{1,0:T(8,128)(2,1)S(1)}, bf16[32,4096]{1,0:T(8,128)(2,1)S(1)}, u32[]{:S(2)}, u32[]{:S(2)}) collective-permute-start(bf16[32,4096]{1,0:T(8,128)(2,1)S(1)} %copy-done.10), channel_id=1, source_target_pairs={{0,6},{1,7},{2,4},{3,5},{4,2},{5,3},{6,0},{7,1},{8,14},{9,15},{10,... | collective-permute-start | bytes 786440 | tf_op jit(solution)/shard_map/ppermute | solution.py:368
  27.7 2.1 %copy-start.8 = (bf16[784,128]{1,0:T(8,128)(2,1)}, bf16[784,128]{1,0:T(8,128)(2,1)S(1)}, u32[]{:S(2)}) copy-start(bf16[784,128]{1,0:T(8,128)(2,1)S(1)} %collective-permute-done.7.refs_8_.refs_13_) | copy-start | bytes 602116
  27.7 28.3 %collective-permute-start.10 = (bf16[32,4096]{1,0:T(8,128)(2,1)S(1)}, bf16[32,4096]{1,0:T(8,128)(2,1)S(1)}, u32[]{:S(2)}, u32[]{:S(2)}) collective-permute-start(bf16[32,4096]{1,0:T(8,128)(2,1)S(1)} %copy-done.10), channel_id=1, source_target_pairs={{0,4},{1,5},{2,6},{3,7},{4,0},{5,1},{6,2},{7,3},{8,12},{9,13},{10,... | collective-permute-start | bytes 786440 | tf_op jit(solution)/shard_map/ppermute | solution.py:368
  28.8 1.0 %copy-start.9 = (bf16[784,128]{1,0:T(8,128)(2,1)}, bf16[784,128]{1,0:T(8,128)(2,1)S(1)}, u32[]{:S(2)}) copy-start(bf16[784,128]{1,0:T(8,128)(2,1)S(1)} %collective-permute-done.8.refs_9_.refs_14_) | copy-start | bytes 602116
  28.8 27.3 %collective-permute-start.9 = (bf16[32,4096]{1,0:T(8,128)(2,1)S(1)}, bf16[32,4096]{1,0:T(8,128)(2,1)S(1)}, u32[]{:S(2)}, u32[]{:S(2)}) collective-permute-start(bf16[32,4096]{1,0:T(8,128)(2,1)S(1)} %copy-done.10), channel_id=1, source_target_pairs={{0,2},{1,3},{2,0},{3,1},{4,6},{5,7},{6,4},{7,5},{8,10},{9,11},{10,... | collective-permute-start | bytes 786440 | tf_op jit(solution)/shard_map/ppermute | solution.py:368
  29.8 0.8 copy-start.5
  58.5 25.8 %collective-permute-start.15 = (f32[32,512]{1,0:T(8,128)S(1)}, f32[32,512]{1,0:T(8,128)S(1)}, u32[]{:S(2)}, u32[]{:S(2)}) collective-permute-start(f32[32,512]{1,0:T(8,128)S(1)} %get-tuple-element.31), channel_id=1, source_target_pairs={{0,6},{1,7},{2,4},{3,5},{4,2},{5,3},{6,0},{7,1},{8,14},{9,15},{10,... | collective-permute-start | bytes 196616 | tf_op jit(solution)/shard_map/ppermute | solution.py:368
  60.1 24.2 %collective-permute-start.14 = (f32[32,512]{1,0:T(8,128)S(1)}, f32[32,512]{1,0:T(8,128)S(1)}, u32[]{:S(2)}, u32[]{:S(2)}) collective-permute-start(f32[32,512]{1,0:T(8,128)S(1)} %get-tuple-element.32), channel_id=1, source_target_pairs={{0,4},{1,5},{2,6},{3,7},{4,0},{5,1},{6,2},{7,3},{8,12},{9,13},{10,... | collective-permute-start | bytes 196616 | tf_op jit(solution)/shard_map/ppermute | solution.py:368
  61.1 23.3 %collective-permute-start.13 = (f32[32,512]{1,0:T(8,128)S(1)}, f32[32,512]{1,0:T(8,128)S(1)}, u32[]{:S(2)}, u32[]{:S(2)}) collective-permute-start(f32[32,512]{1,0:T(8,128)S(1)} %get-tuple-element.33), channel_id=1, source_target_pairs={{0,2},{1,3},{2,0},{3,1},{4,6},{5,7},{6,4},{7,5},{8,10},{9,11},{10,... | collective-permute-start | bytes 196616 | tf_op jit(solution)/shard_map/ppermute | solution.py:368
  84.3 0.6 copy-start.11
  84.3 0.7 copy-start.12
  84.4 0.7 copy-start.13

commit v4 on v3

--- a/solution.py
+++ b/solution.py
@@ -10,6 +10,7 @@
 KEEP_BLK = 12
 PANEL = 128
 SUB = 8
+GROUP = 64
 EXTRA = 16
 VMEM_LIMIT = 56 * 1024 * 1024
 NT = (((1,), (1,)), ((), ()))
@@ -35,39 +36,33 @@
         count = count + flags_ref[b]
 
 
-def select_kernel(flags_ref, tokens_ref, out_ref, index_ref, tile_ref, chunk_ref, tile_sem, chunk_sem):
+def select_kernel(flags_ref, tokens_ref, out_ref, index_ref, held_ref, sem):
     rows, features = tokens_ref.shape
     blocks = flags_ref.shape[0]
     width = features // blocks
     per_tile = 128 // width
-    chunks = chunk_ref.shape[0]
+    chunks = sem.shape[0]
     step = rows // chunks
-    kept_blocks(flags_ref, index_ref)
-    tiles = []
-    for i in range(KEEP_BLK):
-        start = pl.multiple_of((index_ref[i] // per_tile) * 128, 128)
-        tiles.append(
-            pltpu.make_async_copy(tokens_ref.at[:, pl.ds(start, 128)], tile_ref.at[i], tile_sem.at[i])
-        )
-        tiles[-1].start()
     reads = []
     for c in range(chunks):
-        reads.append(
-            pltpu.make_async_copy(tokens_ref.at[c * step:(c + 1) * step, :], chunk_ref.at[c], chunk_sem.at[c])
-        )
+        part = pl.ds(c * step, step)
+        reads.append(pltpu.make_async_copy(tokens_ref.at[part, :], held_ref.at[part, :], sem.at[c]))
         reads[-1].start()
+    kept_blocks(flags_ref, index_ref)
     row = lax.broadcasted_iota(jnp.int32, (width, 128), 0)
     lane = lax.broadcasted_iota(jnp.int32, (width, 128), 1)
-    for copy in tiles + reads:
+    for copy in reads:
         copy.wait()
     for i in range(KEEP_BLK):
-        inner = (index_ref[i] % per_tile) * width
-        pick = jnp.where(lane == row + inner, 1.0, 0.0).astype(jnp.bfloat16)
-        out_ref[i * width:(i + 1) * width, :] = dot32(pick, tile_ref[i], NT).astype(jnp.bfloat16)
+        b = index_ref[i]
+        start = pl.multiple_of((b // per_tile) * 128, 128)
+        pick = jnp.where(lane == row + (b % per_tile) * width, 1.0, 0.0).astype(jnp.bfloat16)
+        picked = dot32(pick, held_ref[:, pl.ds(start, 128)], NT)
+        out_ref[i * width:(i + 1) * width, :] = picked.astype(jnp.bfloat16)
     total = jnp.zeros((step, 128), jnp.float32)
     for c in range(chunks):
         for f in range(features // 128):
-            piece = chunk_ref[c, :, f * 128:(f + 1) * 128].astype(jnp.float32)
+            piece = held_ref[c * step:(c + 1) * step, f * 128:(f + 1) * 128].astype(jnp.float32)
             total += piece * piece
     squares = jnp.sum(total)
     hi, mid, low = split3(jnp.full((EXTRA, rows), squares, jnp.float32))
@@ -95,9 +90,7 @@
         out_specs=pl.BlockSpec(memory_space=pltpu.VMEM),
         scratch_shapes=[
             pltpu.SMEM((blocks + 1,), jnp.int32),
-            pltpu.VMEM((KEEP_BLK, rows, 128), jnp.bfloat16),
-            pltpu.VMEM((chunks, rows // chunks, features), jnp.bfloat16),
-            pltpu.SemaphoreType.DMA((KEEP_BLK,)),
+            pltpu.VMEM((rows, features), jnp.bfloat16),
             pltpu.SemaphoreType.DMA((chunks,)),
         ],
         compiler_params=pltpu.CompilerParams(vmem_limit_bytes=VMEM_LIMIT),
@@ -120,53 +113,71 @@
     return terms[0]
 
 
-def sweep_small(block):
+def solve_small(block, base, rows):
     entry = {}
     for j in range(SUB):
-        column = lane_column(block[0], block[1] + j)
+        column = lane_column(block, base + j)
         for i in range(j + 1):
             entry[i, j] = sublane_row(column, i)
+    rows = list(rows)
     r = pl.reciprocal(entry[0, 0], approx=True)
+    scaled = {}
     for t in range(SUB):
         after = None
         if t + 1 < SUB:
             square = entry[t, t + 1] * entry[t, t + 1]
             after = pl.reciprocal(entry[t + 1, t + 1] - square * r, approx=True)
-        line = [entry[min(i, t), max(i, t)] for i in range(SUB)]
-        scaled = [line[i] * r for i in range(SUB)]
-        for j in range(SUB):
-            for i in range(j + 1):
-                if i != t and j != t:
-                    entry[i, j] = entry[i, j] - line[i] * scaled[j]
-        for i in range(SUB):
-            entry[min(i, t), max(i, t)] = -r if i == t else scaled[i]
+        for j in range(t + 1, SUB):
+            scaled[t, j] = entry[t, j] * r
+        for j in range(t + 1, SUB):
+            for i in range(t + 1, j + 1):
+                entry[i, j] = entry[i, j] - entry[t, i] * scaled[t, j]
+            rows[j] = rows[j] - scaled[t, j] * rows[t]
+        rows[t] = rows[t] * r
         r = after
-    return entry
-
-
-def invert_panel(block):
-    size = block.shape[0]
-    count = size // SUB
-    sub = lax.broadcasted_iota(jnp.int32, (SUB, 128), 0)
-    lane = lax.broadcasted_iota(jnp.int32, (SUB, 128), 1)
-    rows = [block[i * SUB:(i + 1) * SUB, :] for i in range(count)]
+    for t in reversed(range(SUB)):
+        for j in range(t):
+            rows[j] = rows[j] - scaled[j, t] * rows[t]
+    return rows
+
+
+def invert_rows(rows, first, sub, lane, beside):
+    count = len(rows)
     for s in range(count):
-        base = s * SUB
+        base = (first + s) * SUB
         inside = (lane >= base) & (lane < base + SUB)
-        entry = sweep_small((rows[s], base))
         pivot_rows = jnp.where(inside, jnp.where(lane == sub + base, 1.0, 0.0), rows[s])
-        spread_in = [sublane_row(pivot_rows, j) for j in range(SUB)]
-        spread = [
-            tree_sum([entry[min(i, j), max(i, j)] * spread_in[j] for j in range(SUB)]) for i in range(SUB)
-        ]
+        spread = solve_small(rows[s], base, [sublane_row(pivot_rows, j) for j in range(SUB)])
         for i in [(s + d) % count for d in range(1, count)]:
             change = tree_sum([lane_column(rows[i], base + j) * spread[j] for j in range(SUB)])
-            rows[i] = jnp.where(inside, 0.0, rows[i]) + change
+            rows[i] = jnp.where(inside, 0.0, rows[i]) - change
         new = spread[SUB - 1]
         for j in range(SUB - 1):
             new = jnp.where(sub == j, spread[j], new)
-        rows[s] = -new
-    return jnp.concatenate(rows, axis=0)
+        rows[s] = new
+        if beside:
+            beside.pop(0)()
+    return rows
+
+
+def invert_panel(block, beside):
+    size = block.shape[0]
+    sub = lax.broadcasted_iota(jnp.int32, (SUB, 128), 0)
+    lane = lax.broadcasted_iota(jnp.int32, (SUB, 128), 1)
+    row_at = lax.broadcasted_iota(jnp.int32, (size, size), 0) // GROUP
+    lane_at = lax.broadcasted_iota(jnp.int32, (size, size), 1) // GROUP
+    for g in range(size // GROUP):
+        low = g * GROUP
+        rows = [block[low + i:low + i + SUB, :] for i in range(0, GROUP, SUB)]
+        rows = invert_rows(rows, low // SUB, sub, lane, beside)
+        group = jnp.concatenate(rows, axis=0)
+        parts = [jnp.zeros((low, size), jnp.float32)] * (g > 0) + [group]
+        parts += [jnp.zeros((size - low - GROUP, size), jnp.float32)] * (low + GROUP < size)
+        full = jnp.concatenate(parts, axis=0)
+        column = jnp.where((lane_at == g) & (row_at != g), block, 0.0)
+        kept = jnp.where((lane_at == g) | (row_at == g), 0.0, block)
+        block = kept + full - dot32(wide_left(column), wide_right(full), NN)
+    return block
 
 
 def wide_left(x):
@@ -189,9 +200,16 @@
     def _(p):
         at = pl.multiple_of(p * PANEL, PANEL)
         here = pl.ds(at, PANEL)
-        inverse = invert_panel(a_ref[here, here] - dot32(left_ref[here, :], right_ref[:, here], NN))
+
+        def update(r, c, half):
+            a_ref[r:r + half, c:c + 256] -= dot32(left_ref[r:r + half, :], right_ref[:, c:c + 256], NN)
+
+        beside = []
         for c in range(0, kept, 256):
-            a_ref[:, c:c + 256] -= dot32(left_ref[...], right_ref[:, c:c + 256], NN)
+            for r in range(0, kept, kept // 2):
+                beside += [functools.partial(update, r, c, kept // 2), lambda: None]
+        start = a_ref[here, here] - dot32(left_ref[here, :], right_ref[:, here], NN)
+        inverse = invert_panel(start, beside)
         column = jnp.where((row >= at) & (row < at + PANEL), 0.0, a_ref[:, here])
         left_ref[...] = wide_left(column)
         a_ref[:, here] = jnp.zeros((kept, PANEL), jnp.float32)
@@ -307,19 +325,20 @@
     copies = place_pieces(pieces, all_ref, sem)
     kept_blocks(flags_ref, index_ref)
     wide_ref[...] = jnp.zeros((own, features), jnp.float32)
-    split = [split3(part[...]) for part in projected]
-    left = jnp.concatenate([jnp.concatenate([s[i] for s in split], axis=1) for i in range(3)], axis=0)
-    fetch.wait()
+    whole = jnp.concatenate([part[...] for part in projected], axis=1)
+    left = jnp.concatenate(split3(whole), axis=0)
     for copy in copies:
         copy.wait()
-    right = dot32(left, all_ref[:kept, :], NT)
-    right = right[:own] + right[own:2 * own] + right[2 * own:]
+    right = dot32(all_ref[:kept, :], left, NT)
+    right = right[:, :own] + right[:, own:2 * own] + right[:, 2 * own:]
     hi, mid, low = split3(right)
+    fetch.wait()
     ihi, imid, ilow = split3(held_ref[...])
-    first = dot32(jnp.concatenate([hi, mid, low], axis=0), ihi, NN)
-    second = dot32(jnp.concatenate([hi, mid], axis=0), imid, NN)
-    third = dot32(hi, ilow, NN)
-    answer = first[:own] + first[own:2 * own] + second[:own] + first[2 * own:] + second[own:] + third
+    first = dot32(ihi, jnp.concatenate([hi, mid, low], axis=1), NN)
+    second = dot32(imid, jnp.concatenate([hi, mid], axis=1), NN)
+    third = dot32(ilow, hi, NN)
+    answer = first[:, 2 * own:] + second[:, own:] + third + first[:, own:2 * own] + second[:, :own] + first[:, :own]
+    answer = answer.T
     place = lax.broadcasted_iota(jnp.int32, (own, 128), 1) // width
     for i in range(KEEP_BLK):
         b = index_ref[i]

time: 92.4 us -> 97.9 us (1.060)
  Pallas kernels: 59 us -> 64.5 us
    pallas_call x1, Pallas kernels: 25.5 us -> 27.7 us  [first_half(): pl.pallas_call(functools.partial(first_kernel, float(features), rows, las...]
    pallas_call x1, Pallas kernels: 22.3 us -> 24.6 us  [second_half(): pl.pallas_call(functools.partial(second_kernel, first), out_shape=jax.Sha...]
    pallas_call x1, Pallas kernels: 6.93 us -> 8.47 us  [apply_inverse(): pl.pallas_call(functools.partial(apply_kernel, chips), out_shape=jax.Shap...]
where the time goes in v4:
time: 97.9 us; the launch traced here: 97.7 us
  Pallas kernels  64.5 us (66%)
  starting transfers between devices  15.7 us (16%)
  waiting for transfers between devices  13.2 us (13%)
  local copies, waits for them, and re-layouts  2.18 us (2%)
  matrix products  1.67 us (2%)
    pallas_call x1, Pallas kernels, first_half(): pl.pallas_call(functools.partial(first_kernel, float(features), rows, las...  27.7 us
    pallas_call x1, Pallas kernels, second_half(): pl.pallas_call(functools.partial(second_kernel, first), out_shape=jax.Sha...  24.6 us
    ppermute x16, starting transfers between devices, swap(): return lax.ppermute(x, 'dp', [(d, d ^ k) for d in range(n)])  15.7 us
    ppermute x16, waiting for transfers between devices, swap(): return lax.ppermute(x, 'dp', [(d, d ^ k) for d in range(n)])  13.2 us
    pallas_call x1, Pallas kernels, apply_inverse(): pl.pallas_call(functools.partial(apply_kernel, chips), out_shape=jax.Shap...  8.47 us
    pallas_call x1, Pallas kernels, select_kept(): pl.pallas_call(select_kernel, out_shape=jax.ShapeDtypeStruct((kept + EXTR...  3.75 us
  transfers between devices with their start and end apart: 16, of which 3 were waited for; matrix products, arithmetic and copies ran while one was open for 0% of the time, Pallas kernels for 57%

profile of v4, /device:TPU:0, one launch (start us, length us, event | category | flops | bytes accessed | tf_op | source)
XLA Modules:
  0.0 97.7 jit_solution(15118356654051761324)
XLA Ops:
  0.0 0.0 copy-start.10
  0.0 0.5 collective-permute-start.12
  0.5 3.7 %select_kept.1.refs_0_.refs_5_ = bf16[784,256]{1,0:T(8,128)(2,1)} custom-call(s32[64]{0:T(128)} %flags_ref.3, bf16[256,4096]{1,0:T(8,128)(2,1)} %tokens_ref.1), custom_call_target="tpu_custom_call" | custom-call | tf_op jit(solution)/shard_map/select_kept/pallas_call | solution.py:83
  4.2 2.7 %collective-permute-start.3 = (bf16[784,256]{1,0:T(8,128)(2,1)}, bf16[784,256]{1,0:T(8,128)(2,1)S(1)}, u32[]{:S(2)}, u32[]{:S(2)}) collective-permute-start(bf16[784,256]{1,0:T(8,128)(2,1)} %select_kept.1.refs_0_.refs_5_), channel_id=1, source_target_pairs={{0,4},{1,5},{2,6},{3,7},{4,0},{5,1},{6,2},{7,3},{8,12},{9,13},{10,... | collective-permute-start | bytes 1204232 | tf_op jit(solution)/shard_map/ppermute | solution.py:387
  6.9 1.5 %collective-permute-start.1 = (bf16[784,256]{1,0:T(8,128)(2,1)}, bf16[784,256]{1,0:T(8,128)(2,1)S(1)}, u32[]{:S(2)}, u32[]{:S(2)}) collective-permute-start(bf16[784,256]{1,0:T(8,128)(2,1)} %select_kept.1.refs_0_.refs_5_), channel_id=1, source_target_pairs={{0,2},{1,3},{2,0},{3,1},{4,6},{5,7},{6,4},{7,5},{8,10},{9,11},{10,... | collective-permute-start | bytes 1204232 | tf_op jit(solution)/shard_map/ppermute | solution.py:387
  8.4 0.0 collective-permute-start
  8.4 8.5 %collective-permute-done.3.refs_4_.refs_9_ = bf16[784,256]{1,0:T(8,128)(2,1)S(1)} collective-permute-done((bf16[784,256]{1,0:T(8,128)(2,1)}, bf16[784,256]{1,0:T(8,128)(2,1)S(1)}, u32[]{:S(2)}, u32[]{:S(2)}) %collective-permute-start.3) | collective-permute-done | bytes 401440 | tf_op jit(solution)/shard_map/ppermute | solution.py:387
  17.0 0.0 copy-start.1
  17.0 1.8 %collective-permute-start.6 = (bf16[784,128]{1,0:T(8,128)(2,1)S(1)}, bf16[784,128]{1,0:T(8,128)(2,1)S(1)}, u32[]{:S(2)}, u32[]{:S(2)}) collective-permute-start(bf16[784,128]{1,0:T(8,128)(2,1)S(1)} %slice.25), channel_id=1, source_target_pairs={{0,2},{1,3},{2,0},{3,1},{4,6},{5,7},{6,4},{7,5},{8,10},{9,11},{10,... | collective-permute-start | bytes 602120 | tf_op jit(solution)/shard_map/ppermute | solution.py:387
  18.8 0.0 collective-permute-done.1.refs_2_.refs_7_
  18.8 0.0 copy-start.2
  18.8 0.0 copy-start
  18.8 1.6 %collective-permute-start.5 = (bf16[784,128]{1,0:T(8,128)(2,1)S(1)}, bf16[784,128]{1,0:T(8,128)(2,1)S(1)}, u32[]{:S(2)}, u32[]{:S(2)}) collective-permute-start(bf16[784,128]{1,0:T(8,128)(2,1)S(1)} %slice.24), channel_id=1, source_target_pairs={{0,4},{1,5},{2,6},{3,7},{4,0},{5,1},{6,2},{7,3},{8,12},{9,13},{10,... | collective-permute-start | bytes 602120 | tf_op jit(solution)/shard_map/ppermute | solution.py:387
  20.4 0.0 collective-permute-start.4
  20.4 3.4 %collective-permute-done.6.refs_7_.refs_12_ = bf16[784,128]{1,0:T(8,128)(2,1)S(1)} collective-permute-done((bf16[784,128]{1,0:T(8,128)(2,1)S(1)}, bf16[784,128]{1,0:T(8,128)(2,1)S(1)}, u32[]{:S(2)}, u32[]{:S(2)}) %collective-permute-start.6) | collective-permute-done | bytes 200736 | tf_op jit(solution)/shard_map/ppermute | solution.py:387
  23.7 0.0 copy-start.6
  23.7 1.3 %collective-permute-done.5.refs_6_.refs_11_ = bf16[784,128]{1,0:T(8,128)(2,1)S(1)} collective-permute-done((bf16[784,128]{1,0:T(8,128)(2,1)S(1)}, bf16[784,128]{1,0:T(8,128)(2,1)S(1)}, u32[]{:S(2)}, u32[]{:S(2)}) %collective-permute-start.5) | collective-permute-done | bytes 200736 | tf_op jit(solution)/shard_map/ppermute | solution.py:387
  25.0 0.0 copy-start.7
  25.0 0.0 collective-permute-start.7
  25.0 0.5 collective-permute-start.8
  25.6 0.0 collective-permute-done.refs_1_.refs_6_
  25.6 0.0 copy-start.3
  25.6 0.1 collective-permute-start.2
  25.6 0.0 collective-permute-done.4.refs_5_.refs_10_
  25.6 0.0 copy-done.10
  25.6 0.0 copy-start.4
  25.6 1.6 %collective-permute-start.11 = (bf16[32,4096]{1,0:T(8,128)(2,1)S(1)}, bf16[32,4096]{1,0:T(8,128)(2,1)S(1)}, u32[]{:S(2)}, u32[]{:S(2)}) collective-permute-start(bf16[32,4096]{1,0:T(8,128)(2,1)S(1)} %copy-done.10), channel_id=1, source_target_pairs={{0,6},{1,7},{2,4},{3,5},{4,2},{5,3},{6,0},{7,1},{8,14},{9,15},{10,... | collective-permute-start | bytes 786440 | tf_op jit(solution)/shard_map/ppermute | solution.py:387
  27.2 0.0 collective-permute-done.7.refs_8_.refs_13_
  27.2 1.1 %collective-permute-start.10 = (bf16[32,4096]{1,0:T(8,128)(2,1)S(1)}, bf16[32,4096]{1,0:T(8,128)(2,1)S(1)}, u32[]{:S(2)}, u32[]{:S(2)}) collective-permute-start(bf16[32,4096]{1,0:T(8,128)(2,1)S(1)} %copy-done.10), channel_id=1, source_target_pairs={{0,4},{1,5},{2,6},{3,7},{4,0},{5,1},{6,2},{7,3},{8,12},{9,13},{10,... | collective-permute-start | bytes 786440 | tf_op jit(solution)/shard_map/ppermute | solution.py:387
  28.3 0.0 collective-permute-done.8.refs_9_.refs_14_
  28.3 0.9 collective-permute-start.9
  29.2 0.0 collective-permute-done.2.refs_3_.refs_8_
  29.2 0.0 copy-done.1
  29.2 0.0 copy-done.2
  29.2 0.0 copy-done.6
  29.2 0.0 copy-done.7
  29.2 0.0 copy-done.3
  29.2 0.0 copy-done.4
  29.2 0.0 copy-done.8
  29.3 0.0 copy-done.9
  29.3 0.0 copy-start.5
  29.3 0.8 copy-done.5
  30.0 27.7 %gram_and_first_panels.1 = (f32[768,768]{1,0:T(8,128)}, f32[8,128]{1,0:T(8,128)}) custom-call(bf16[784,256]{1,0:T(8,128)(2,1)} %select_kept.1.refs_0_.refs_5_, bf16[784,256]{1,0:T(8,128)(2,1)} %copy-done.3, bf16[784,256]{1,0:T(8,128)(2,1)} %copy-done.2, bf16[784,256]{1,0:T(8,128)(2,1)} %copy-done.5, bf16[784,256]{1,0:T(8,128)(2,1)} %copy-done.1, ...), custom_call_target="tpu_custom_call" | custom-call | tf_op jit(solution)/shard_map/gram_and_first_panels/pallas_call | solution.py:272
  57.8 0.0 collective-permute-done.11
  57.8 0.0 collective-permute-done.10
  57.8 0.0 collective-permute-done.9
  57.8 0.0 collective-permute-done.12
  57.9 0.0 copy-done
  57.9 0.8 fusion.1
  58.8 0.8 fusion.2
  59.6 0.6 fusion
  60.3 1.6 %collective-permute-start.15 = (f32[32,512]{1,0:T(8,128)S(1)}, f32[32,512]{1,0:T(8,128)S(1)}, u32[]{:S(2)}, u32[]{:S(2)}) collective-permute-start(f32[32,512]{1,0:T(8,128)S(1)} %get-tuple-element.31), channel_id=1, source_target_pairs={{0,6},{1,7},{2,4},{3,5},{4,2},{5,3},{6,0},{7,1},{8,14},{9,15},{10,... | collective-permute-start | bytes 196616 | tf_op jit(solution)/shard_map/ppermute | solution.py:387
  61.9 1.0 %collective-permute-start.14 = (f32[32,512]{1,0:T(8,128)S(1)}, f32[32,512]{1,0:T(8,128)S(1)}, u32[]{:S(2)}, u32[]{:S(2)}) collective-permute-start(f32[32,512]{1,0:T(8,128)S(1)} %get-tuple-element.32), channel_id=1, source_target_pairs={{0,4},{1,5},{2,6},{3,7},{4,0},{5,1},{6,2},{7,3},{8,12},{9,13},{10,... | collective-permute-start | bytes 196616 | tf_op jit(solution)/shard_map/ppermute | solution.py:387
  62.8 0.9 collective-permute-start.13
  63.8 24.6 %last_panels.1.refs_4_ = f32[768,768]{1,0:T(8,128)} custom-call(f32[768,768]{1,0:T(8,128)} %get-tuple-element.29.a_ref, f32[8,128]{1,0:T(8,128)} %get-tuple-element.30.scale_ref), custom_call_target="tpu_custom_call" | custom-call | tf_op jit(solution)/shard_map/last_panels/pallas_call | solution.py:300
  88.3 0.0 collective-permute-done.15.refs_3_
  88.3 0.0 collective-permute-done.14.refs_2_
  88.4 0.0 copy-start.12
  88.4 0.0 collective-permute-done.13.refs_1_
  88.4 0.0 copy-start.13
  88.4 0.6 copy-done.11
  89.0 0.0 copy-done.12
  89.0 0.0 copy-done.13
  89.0 8.5 %apply_inverse.1 = bf16[32,4096]{1,0:T(8,128)(2,1)} custom-call(s32[64]{0:T(128)} %flags_ref.3, f32[32,512]{1,0:T(8,128)} %get-tuple-element.34.refs_0_, f32[32,512]{1,0:T(8,128)} %copy-done.13, f32[32,512]{1,0:T(8,128)} %copy-done.12, f32[32,512]{1,0:T(8,128)} %copy-done.11, f32[768,768]{1,0:T(8,128)} %last_panels.1.refs_4_, ...), custom_call_target="tpu_custom_call" | custom-call | tf_op jit(solution)/shard_map/apply_inverse/pallas_call | solution.py:364
  (10 shorter events, 0.1 us)
Async XLA Ops:
  0.0 25.6 %copy-start.10 = (bf16[32,4096]{1,0:T(8,128)(2,1)S(1)}, bf16[32,4096]{1,0:T(8,128)(2,1)}, u32[]{:S(2)}) copy-start(bf16[32,4096]{1,0:T(8,128)(2,1)} %param.4) | copy-start | bytes 786436
  0.0 57.8 %collective-permute-start.12 = (bf16[256,4096]{1,0:T(8,128)(2,1)}, bf16[256,4096]{1,0:T(8,128)(2,1)S(1)}, u32[]{:S(2)}, u32[]{:S(2)}) collective-permute-start(bf16[256,4096]{1,0:T(8,128)(2,1)} %tokens_ref.1), channel_id=1, source_target_pairs={{0,1},{1,0},{2,3},{3,2},{4,5},{5,4},{6,7},{7,6},{8,9},{9,8},{10,11... | collective-permute-start | bytes 6291464 | tf_op jit(solution)/shard_map/ppermute | solution.py:387
  4.2 12.8 %collective-permute-start.3 = (bf16[784,256]{1,0:T(8,128)(2,1)}, bf16[784,256]{1,0:T(8,128)(2,1)S(1)}, u32[]{:S(2)}, u32[]{:S(2)}) collective-permute-start(bf16[784,256]{1,0:T(8,128)(2,1)} %select_kept.1.refs_0_.refs_5_), channel_id=1, source_target_pairs={{0,4},{1,5},{2,6},{3,7},{4,0},{5,1},{6,2},{7,3},{8,12},{9,13},{10,... | collective-permute-start | bytes 1204232 | tf_op jit(solution)/shard_map/ppermute | solution.py:387
  6.9 11.8 %collective-permute-start.1 = (bf16[784,256]{1,0:T(8,128)(2,1)}, bf16[784,256]{1,0:T(8,128)(2,1)S(1)}, u32[]{:S(2)}, u32[]{:S(2)}) collective-permute-start(bf16[784,256]{1,0:T(8,128)(2,1)} %select_kept.1.refs_0_.refs_5_), channel_id=1, source_target_pairs={{0,2},{1,3},{2,0},{3,1},{4,6},{5,7},{6,4},{7,5},{8,10},{9,11},{10,... | collective-permute-start | bytes 1204232 | tf_op jit(solution)/shard_map/ppermute | solution.py:387
  8.4 17.1 %collective-permute-start = (bf16[784,256]{1,0:T(8,128)(2,1)}, bf16[784,256]{1,0:T(8,128)(2,1)S(1)}, u32[]{:S(2)}, u32[]{:S(2)}) collective-permute-start(bf16[784,256]{1,0:T(8,128)(2,1)} %select_kept.1.refs_0_.refs_5_), channel_id=1, source_target_pairs={{0,1},{1,0},{2,3},{3,2},{4,5},{5,4},{6,7},{7,6},{8,9},{9,8},{10,11... | collective-permute-start | bytes 1204232 | tf_op jit(solution)/shard_map/ppermute | solution.py:387
  17.0 12.2 %copy-start.1 = (bf16[784,256]{1,0:T(8,128)(2,1)}, bf16[784,256]{1,0:T(8,128)(2,1)S(1)}, u32[]{:S(2)}) copy-start(bf16[784,256]{1,0:T(8,128)(2,1)S(1)} %collective-permute-done.3.refs_4_.refs_9_) | copy-start | bytes 1204228
  17.0 6.8 %collective-permute-start.6 = (bf16[784,128]{1,0:T(8,128)(2,1)S(1)}, bf16[784,128]{1,0:T(8,128)(2,1)S(1)}, u32[]{:S(2)}, u32[]{:S(2)}) collective-permute-start(bf16[784,128]{1,0:T(8,128)(2,1)S(1)} %slice.25), channel_id=1, source_target_pairs={{0,2},{1,3},{2,0},{3,1},{4,6},{5,7},{6,4},{7,5},{8,10},{9,11},{10,... | collective-permute-start | bytes 602120 | tf_op jit(solution)/shard_map/ppermute | solution.py:387
  18.8 10.4 %copy-start.2 = (bf16[784,256]{1,0:T(8,128)(2,1)}, bf16[784,256]{1,0:T(8,128)(2,1)S(1)}, u32[]{:S(2)}) copy-start(bf16[784,256]{1,0:T(8,128)(2,1)S(1)} %collective-permute-done.1.refs_2_.refs_7_) | copy-start | bytes 1204228
  18.8 39.1 %copy-start = (bf16[256,4096]{1,0:T(8,128)(2,1)S(1)}, bf16[256,4096]{1,0:T(8,128)(2,1)}, u32[]{:S(2)}) copy-start(bf16[256,4096]{1,0:T(8,128)(2,1)} %tokens_ref.1) | copy-start | bytes 6291460
  18.8 6.2 %collective-permute-start.5 = (bf16[784,128]{1,0:T(8,128)(2,1)S(1)}, bf16[784,128]{1,0:T(8,128)(2,1)S(1)}, u32[]{:S(2)}, u32[]{:S(2)}) collective-permute-start(bf16[784,128]{1,0:T(8,128)(2,1)S(1)} %slice.24), channel_id=1, source_target_pairs={{0,4},{1,5},{2,6},{3,7},{4,0},{5,1},{6,2},{7,3},{8,12},{9,13},{10,... | collective-permute-start | bytes 602120 | tf_op jit(solution)/shard_map/ppermute | solution.py:387
  20.4 5.2 %collective-permute-start.4 = (bf16[784,256]{1,0:T(8,128)(2,1)S(1)}, bf16[784,256]{1,0:T(8,128)(2,1)S(1)}, u32[]{:S(2)}, u32[]{:S(2)}) collective-permute-start(bf16[784,256]{1,0:T(8,128)(2,1)S(1)} %collective-permute-done.3.refs_4_.refs_9_), channel_id=1, source_target_pairs={{0,1},{1,0},{2,3},{3,2},{4,5},{5,4},{6,7},{7,6},{8,9},{9,8},{10,11... | collective-permute-start | bytes 1204232 | tf_op jit(solution)/shard_map/ppermute | solution.py:387
  23.7 5.5 %copy-start.6 = (bf16[784,128]{1,0:T(8,128)(2,1)}, bf16[784,128]{1,0:T(8,128)(2,1)S(1)}, u32[]{:S(2)}) copy-start(bf16[784,128]{1,0:T(8,128)(2,1)S(1)} %collective-permute-done.6.refs_7_.refs_12_) | copy-start | bytes 602116
  25.0 4.2 %copy-start.7 = (bf16[784,128]{1,0:T(8,128)(2,1)}, bf16[784,128]{1,0:T(8,128)(2,1)S(1)}, u32[]{:S(2)}) copy-start(bf16[784,128]{1,0:T(8,128)(2,1)S(1)} %collective-permute-done.5.refs_6_.refs_11_) | copy-start | bytes 602116
  25.0 2.2 %collective-permute-start.7 = (bf16[784,128]{1,0:T(8,128)(2,1)S(1)}, bf16[784,128]{1,0:T(8,128)(2,1)S(1)}, u32[]{:S(2)}, u32[]{:S(2)}) collective-permute-start(bf16[784,128]{1,0:T(8,128)(2,1)S(1)} %collective-permute-done.5.refs_6_.refs_11_), channel_id=1, source_target_pairs={{0,1},{1,0},{2,3},{3,2},{4,5},{5,4},{6,7},{7,6},{8,9},{9,8},{10,11... | collective-permute-start | bytes 602120 | tf_op jit(solution)/shard_map/ppermute | solution.py:387
  25.0 3.2 %collective-permute-start.8 = (bf16[784,128]{1,0:T(8,128)(2,1)S(1)}, bf16[784,128]{1,0:T(8,128)(2,1)S(1)}, u32[]{:S(2)}, u32[]{:S(2)}) collective-permute-start(bf16[784,128]{1,0:T(8,128)(2,1)S(1)} %collective-permute-done.6.refs_7_.refs_12_), channel_id=1, source_target_pairs={{0,1},{1,0},{2,3},{3,2},{4,5},{5,4},{6,7},{7,6},{8,9},{9,8},{10,11... | collective-permute-start | bytes 602120 | tf_op jit(solution)/shard_map/ppermute | solution.py:387
  25.6 3.7 %copy-start.3 = (bf16[784,256]{1,0:T(8,128)(2,1)}, bf16[784,256]{1,0:T(8,128)(2,1)S(1)}, u32[]{:S(2)}) copy-start(bf16[784,256]{1,0:T(8,128)(2,1)S(1)} %collective-permute-done.refs_1_.refs_6_) | copy-start | bytes 1204228
  25.6 3.6 %collective-permute-start.2 = (bf16[784,256]{1,0:T(8,128)(2,1)S(1)}, bf16[784,256]{1,0:T(8,128)(2,1)S(1)}, u32[]{:S(2)}, u32[]{:S(2)}) collective-permute-start(bf16[784,256]{1,0:T(8,128)(2,1)S(1)} %collective-permute-done.1.refs_2_.refs_7_), channel_id=1, source_target_pairs={{0,1},{1,0},{2,3},{3,2},{4,5},{5,4},{6,7},{7,6},{8,9},{9,8},{10,11... | collective-permute-start | bytes 1204232 | tf_op jit(solution)/shard_map/ppermute | solution.py:387
  25.6 3.6 %copy-start.4 = (bf16[784,256]{1,0:T(8,128)(2,1)}, bf16[784,256]{1,0:T(8,128)(2,1)S(1)}, u32[]{:S(2)}) copy-start(bf16[784,256]{1,0:T(8,128)(2,1)S(1)} %collective-permute-done.4.refs_5_.refs_10_) | copy-start | bytes 1204228
  25.6 32.1 %collective-permute-start.11 = (bf16[32,4096]{1,0:T(8,128)(2,1)S(1)}, bf16[32,4096]{1,0:T(8,128)(2,1)S(1)}, u32[]{:S(2)}, u32[]{:S(2)}) collective-permute-start(bf16[32,4096]{1,0:T(8,128)(2,1)S(1)} %copy-done.10), channel_id=1, source_target_pairs={{0,6},{1,7},{2,4},{3,5},{4,2},{5,3},{6,0},{7,1},{8,14},{9,15},{10,... | collective-permute-start | bytes 786440 | tf_op jit(solution)/shard_map/ppermute | solution.py:387
  27.2 2.1 %copy-start.8 = (bf16[784,128]{1,0:T(8,128)(2,1)}, bf16[784,128]{1,0:T(8,128)(2,1)S(1)}, u32[]{:S(2)}) copy-start(bf16[784,128]{1,0:T(8,128)(2,1)S(1)} %collective-permute-done.7.refs_8_.refs_13_) | copy-start | bytes 602116
  27.2 30.6 %collective-permute-start.10 = (bf16[32,4096]{1,0:T(8,128)(2,1)S(1)}, bf16[32,4096]{1,0:T(8,128)(2,1)S(1)}, u32[]{:S(2)}, u32[]{:S(2)}) collective-permute-start(bf16[32,4096]{1,0:T(8,128)(2,1)S(1)} %copy-done.10), channel_id=1, source_target_pairs={{0,4},{1,5},{2,6},{3,7},{4,0},{5,1},{6,2},{7,3},{8,12},{9,13},{10,... | collective-permute-start | bytes 786440 | tf_op jit(solution)/shard_map/ppermute | solution.py:387
  28.3 1.0 %copy-start.9 = (bf16[784,128]{1,0:T(8,128)(2,1)}, bf16[784,128]{1,0:T(8,128)(2,1)S(1)}, u32[]{:S(2)}) copy-start(bf16[784,128]{1,0:T(8,128)(2,1)S(1)} %collective-permute-done.8.refs_9_.refs_14_) | copy-start | bytes 602116
  28.3 29.5 %collective-permute-start.9 = (bf16[32,4096]{1,0:T(8,128)(2,1)S(1)}, bf16[32,4096]{1,0:T(8,128)(2,1)S(1)}, u32[]{:S(2)}, u32[]{:S(2)}) collective-permute-start(bf16[32,4096]{1,0:T(8,128)(2,1)S(1)} %copy-done.10), channel_id=1, source_target_pairs={{0,2},{1,3},{2,0},{3,1},{4,6},{5,7},{6,4},{7,5},{8,10},{9,11},{10,... | collective-permute-start | bytes 786440 | tf_op jit(solution)/shard_map/ppermute | solution.py:387
  29.3 0.8 copy-start.5
  60.3 28.1 %collective-permute-start.15 = (f32[32,512]{1,0:T(8,128)S(1)}, f32[32,512]{1,0:T(8,128)S(1)}, u32[]{:S(2)}, u32[]{:S(2)}) collective-permute-start(f32[32,512]{1,0:T(8,128)S(1)} %get-tuple-element.31), channel_id=1, source_target_pairs={{0,6},{1,7},{2,4},{3,5},{4,2},{5,3},{6,0},{7,1},{8,14},{9,15},{10,... | collective-permute-start | bytes 196616 | tf_op jit(solution)/shard_map/ppermute | solution.py:387
  61.9 26.5 %collective-permute-start.14 = (f32[32,512]{1,0:T(8,128)S(1)}, f32[32,512]{1,0:T(8,128)S(1)}, u32[]{:S(2)}, u32[]{:S(2)}) collective-permute-start(f32[32,512]{1,0:T(8,128)S(1)} %get-tuple-element.32), channel_id=1, source_target_pairs={{0,4},{1,5},{2,6},{3,7},{4,0},{5,1},{6,2},{7,3},{8,12},{9,13},{10,... | collective-permute-start | bytes 196616 | tf_op jit(solution)/shard_map/ppermute | solution.py:387
  62.8 25.5 %collective-permute-start.13 = (f32[32,512]{1,0:T(8,128)S(1)}, f32[32,512]{1,0:T(8,128)S(1)}, u32[]{:S(2)}, u32[]{:S(2)}) collective-permute-start(f32[32,512]{1,0:T(8,128)S(1)} %get-tuple-element.33), channel_id=1, source_target_pairs={{0,2},{1,3},{2,0},{3,1},{4,6},{5,7},{6,4},{7,5},{8,10},{9,11},{10,... | collective-permute-start | bytes 196616 | tf_op jit(solution)/shard_map/ppermute | solution.py:387
  88.3 0.6 copy-start.11
  88.4 0.7 copy-start.12
  88.4 0.7 copy-start.13
